TPU v7x, 32 devices: a whole 2x2x4 slice. The times are simulated.
32 devices in a mesh: slab: 4 (over y, x), tile: 8 (over z, core).
Axes of the slice: x: 2, y: 2, z: 4, core: 2. Of those that a mesh axis runs over, the one named last changes fastest.
Arguments:
- features: bfloat16 [65536, 128], P(('slab', 'tile')), may hold values from -6 to 6
- conv_weight: bfloat16 [27, 128, 128], replicated, may hold values from -0.15625 to 0.15625
- down_weight: bfloat16 [8, 128, 128], replicated, may hold values from -0.25 to 0.25
- coarse_grad: bfloat16 [16384, 128], P(('slab', 'tile')), may hold values from -6 to 6
- rulebook: int32 [27, 65536], P(None, ('slab', 'tile')), may hold values from 0 to 3072, as said below
- boundary_rows: int32 [128, 256], P(('slab', 'tile')), may hold values from 0 to 2047, as said below
- parent_code: int32 [65536], P(('slab', 'tile')), may hold values from 0 to 4096, as said below
Outputs:
- coarse: bfloat16 [16384, 128], P(('slab', 'tile'))
- input_grad: float32 [65536, 128], P(('slab', 'tile'))
- conv_grad: float32 [27, 128, 128], replicated
- down_grad: float32 [8, 128, 128], replicated
Inputs may be any that keep to these rules, and one draw needn't show every extreme that they name: `rulebook`: each partition has some number of live blocks of 128 rows, at least one and fewer than 16, at its start; rows of the remaining blocks are dead. For a live row, the centre offset (13) reads the row itself; other entries read a live local row, a received row (2048 to 3071) or the empty row 3072. For each offset and each aligned block of 128 rows of a partition, all entries other than 3072 lie in one aligned block of 128 rows of the extended table. Every entry of a dead row is 3072. `boundary_rows`: entries are live rows of the partition; repeats may occur. `parent_code`: within a partition the live rows with one parent have distinct child positions, at most 4 per parent; the parents of the rows of local block b lie in coarse rows b * 32 to (b + 1) * 32 - 1; dead rows have the code 8 * 512.
All inputs are finite; a program needn't handle non-finite values.
Results may differ from a plain program's by a relative error of at most 0.02.
Values may be sent and summed in bfloat16 or wider, within the bound.
A program may use at most 64 MiB of HBM per device.

v0:
```python
import jax
import jax.numpy as jnp
from jax import lax
from jax.sharding import PartitionSpec as P

BLOCK = 128


def with_halo(shard, sides, width):
    for axis, dim in sides:
        devices, length = (lax.axis_size(axis), shard.shape[dim])
        up = [(i, (i + 1) % devices) for i in range(devices - 1)]
        down = [(j, i) for i, j in up]
        last = lax.slice_in_dim(shard, length - width, length, axis=dim)
        first = lax.slice_in_dim(shard, 0, width, axis=dim)
        before = lax.ppermute(last, axis, up)
        after = lax.ppermute(first, axis, down)
        shard = jnp.concatenate([before, shard, after], axis=dim)
    return shard


def body(features, conv_weight, down_weight, coarse_grad, rulebook, boundary_rows, parent_code):
    row_count = features.shape[0]
    chan_count = features.shape[1]
    coarse_rows = coarse_grad.shape[0]
    out_chans = coarse_grad.shape[1]
    list_len = boundary_rows.shape[1]
    child_count = down_weight.shape[0]
    kernel_count = conv_weight.shape[0]
    block_len = BLOCK
    block_total = row_count // block_len
    ext_len = row_count + 4 * list_len
    table_blocks = ext_len // block_len + 1
    outgoing = features[boundary_rows]
    arrived = with_halo(outgoing[None, None], (("slab", 0), ("tile", 1)), 1)
    received = jnp.stack([arrived[0, 1, 0], arrived[2, 1, 1], arrived[1, 0, 2], arrived[1, 2, 3]])
    extended = jnp.concatenate(
        [
            features,
            received.reshape(4 * list_len, chan_count),
            jnp.zeros((block_len, chan_count), jnp.bfloat16),
        ],
        axis=0,
    )
    ext_flat = extended.reshape(table_blocks, block_len * chan_count)
    book_rows = rulebook.reshape(kernel_count, block_total, block_len)
    book_block = book_rows // block_len
    source = jnp.min(book_block, axis=2)
    inner_idx = book_rows % block_len
    in_block = book_block == source[:, :, None]
    columns = jnp.arange(block_len, dtype=jnp.int32)
    block_ids = jnp.arange(table_blocks, dtype=jnp.int32)

    def block_pick(src_block):
        return src_block[:, None] == block_ids[None, :]

    def row_pick(inner_one, valid_one):
        return (inner_one[:, :, None] == columns[None, None, :]) & valid_one[:, :, None]

    def forward_step(running, pieces):
        src_block, inner_one, valid_one, weight_one = pieces
        picked = jnp.dot(
            block_pick(src_block).astype(jnp.bfloat16), ext_flat, preferred_element_type=jnp.float32
        )
        picked = picked.astype(jnp.bfloat16).reshape(block_total, block_len, chan_count)
        rows_one = jnp.einsum(
            "bij,bjc->bic",
            row_pick(inner_one, valid_one).astype(jnp.bfloat16),
            picked,
            preferred_element_type=jnp.float32,
        )
        rows_one = rows_one.astype(jnp.bfloat16).reshape(row_count, chan_count)
        return (
            running + jnp.dot(rows_one, weight_one, preferred_element_type=jnp.float32),
            rows_one,
        )

    pre_act, gathered = lax.scan(
        forward_step,
        jnp.zeros((row_count, chan_count), jnp.float32),
        (source, inner_idx, in_block, conv_weight),
    )
    hidden = jnp.maximum(pre_act, 0.0).astype(jnp.bfloat16)
    parent = parent_code // 8
    slot_idx = parent_code % 8
    has_parent = parent < coarse_rows
    quarter = coarse_rows // block_total
    local_parent = parent - jnp.arange(row_count, dtype=jnp.int32) // block_len * quarter
    child_hot = (
        local_parent.reshape(block_total, 1, block_len, 1)
        == jnp.arange(quarter, dtype=jnp.int32)[None, :, None, None]
    )
    child_hot = child_hot & (
        slot_idx.reshape(block_total, 1, block_len, 1)
        == jnp.arange(child_count, dtype=jnp.int32)[None, None, None, :]
    )
    child_hot = child_hot & has_parent.reshape(block_total, 1, block_len, 1)
    children = jnp.einsum(
        "bqrs,brc->bqsc",
        child_hot.astype(jnp.bfloat16),
        hidden.reshape(block_total, block_len, chan_count),
        preferred_element_type=jnp.float32,
    )
    children = children.astype(jnp.bfloat16).reshape(coarse_rows, child_count * chan_count)
    down_flat = down_weight.reshape(child_count * chan_count, out_chans)
    coarse = jnp.dot(children, down_flat, preferred_element_type=jnp.float32).astype(jnp.bfloat16)
    down_part = lax.dot_general(
        children, coarse_grad, (((0,), (0,)), ((), ())), preferred_element_type=jnp.float32
    )
    spread_grad = lax.dot_general(
        coarse_grad, down_flat, (((1,), (1,)), ((), ())), preferred_element_type=jnp.float32
    )
    spread_grad = spread_grad.reshape(block_total, quarter, child_count, chan_count)
    hidden_grad = jnp.einsum(
        "bqrs,bqsc->brc",
        child_hot.astype(jnp.float32),
        spread_grad,
        precision=lax.Precision.HIGHEST,
    ).reshape(row_count, chan_count)
    pre_grad = jnp.where(pre_act > 0, hidden_grad, 0.0).astype(jnp.bfloat16)

    def backward_step(ext_total, pieces):
        src_block, inner_one, valid_one, weight_one, rows_one = pieces
        conv_one = lax.dot_general(
            rows_one, pre_grad, (((0,), (0,)), ((), ())), preferred_element_type=jnp.float32
        )
        back_terms = lax.dot_general(
            pre_grad, weight_one, (((1,), (1,)), ((), ())), preferred_element_type=jnp.float32
        )
        back_terms = back_terms.reshape(block_total, block_len, chan_count)
        within = jnp.einsum(
            "bij,bic->bjc",
            row_pick(inner_one, valid_one).astype(jnp.float32),
            back_terms,
            precision=lax.Precision.HIGHEST,
        )
        placed = jnp.einsum(
            "bn,bjc->njc",
            block_pick(src_block).astype(jnp.float32),
            within,
            precision=lax.Precision.HIGHEST,
        )
        return (ext_total + placed, conv_one)

    ext_grad, conv_part = lax.scan(
        backward_step,
        jnp.zeros((table_blocks, block_len, chan_count), jnp.float32),
        (source, inner_idx, in_block, conv_weight, gathered),
    )
    ext_rows = ext_grad.reshape(table_blocks * block_len, chan_count)
    halo_grad = ext_rows[row_count:ext_len].reshape(4, list_len, chan_count)
    coming = with_halo(
        halo_grad[None, None].astype(jnp.bfloat16), (("slab", 0), ("tile", 1)), 1
    ).astype(jnp.float32)
    returned = jnp.stack([coming[2, 1, 0], coming[0, 1, 1], coming[1, 2, 2], coming[1, 0, 3]])
    input_grad = (
        ext_rows[:row_count]
        .at[boundary_rows.reshape(4 * list_len)]
        .add(returned.reshape(4 * list_len, chan_count))
    )
    conv_grad, down_total = lax.psum((conv_part, down_part), ("slab", "tile"))
    return (coarse, input_grad, conv_grad, down_total.reshape(child_count, chan_count, out_chans))


def solution(mesh):
    return jax.shard_map(
        body,
        mesh=mesh,
        in_specs=(
            P(("slab", "tile"), None),
            P(),
            P(),
            P(("slab", "tile"), None),
            P(None, ("slab", "tile")),
            P(("slab", "tile"), None),
            P(("slab", "tile")),
        ),
        out_specs=(P(("slab", "tile"), None), P(("slab", "tile"), None), P(), P()),
        check_vma=False,
    )
```

profile of v0, /device:TPU:0, one launch (start us, length us, event | category | flops | bytes accessed | tf_op | source)
XLA Modules:
  0.0 659.8 jit_solution(6174945210504899184)
XLA Ops:
  12.0 4.9 collective-permute-start
  23.4 6.6 collective-permute-done.1
  39.6 130.2 %while.26 = (s32[]{:T(128)}, f32[2048,128]{1,0:T(8,128)S(1)}, bf16[27,2048,128]{2,1,0:T(8,128)(2,1)}, s32[27,16,128]{2,1,0:T(8,128)}, pred[27,16,128]{2,1,0:T(8,...) while((s32[]{:T(128)}, f32[2048,128]{1,0:T(8,128)S(1)}, ...), condition=%wide.region_2.3_spmd.clone, body=%wide.region_1.2_spmd.clone.sunk | while | flops 148898192 | bytes 7175483 | solution.py:78
  170.8 310.9 %while.27 = (s32[]{:T(128)}, f32[25,128,128]{2,0,1:T(8,128)}, f32[27,128,128]{2,1,0:T(8,128)}, s32[27,16]{1,0:T(8,128)S(1)}, s32[27,16,128]{2,1,0:T(8,128)}, /*i...) while((s32[]{:T(128)}, f32[25,128,128]{2,0,1:T(8,128)}, ...), condition=%wide.region_4.5_spmd.clone, body=%wide.region_3.4_spmd.clone.sunk | while | flops 616857984 | bytes 11272003 | solution.py:145
  185.8 4.6 select_add_fusion.2
  197.4 4.6 select_add_fusion.2
  209.0 4.6 select_add_fusion.2
  220.5 4.6 select_add_fusion.2
  232.1 4.6 select_add_fusion.2
  243.7 4.6 select_add_fusion.2
  255.3 4.6 select_add_fusion.2
  266.8 4.6 select_add_fusion.2
  278.4 4.6 select_add_fusion.2
  290.0 4.6 select_add_fusion.2
  301.6 4.6 select_add_fusion.2
  313.1 4.6 select_add_fusion.2
  324.7 4.6 select_add_fusion.2
  336.3 4.6 select_add_fusion.2
  347.9 4.6 select_add_fusion.2
  359.4 4.6 select_add_fusion.2
  371.0 4.6 select_add_fusion.2
  382.6 4.6 select_add_fusion.2
  394.2 4.6 select_add_fusion.2
  405.7 4.6 select_add_fusion.2
  417.3 4.6 select_add_fusion.2
  428.9 4.6 select_add_fusion.2
  452.0 4.6 select_add_fusion.2
  475.2 4.6 select_add_fusion.2
  497.1 8.2 %collective-permute-start.6 = (bf16[3,1,4,256,128]{4,3,2,1,0:T(8,128)(2,1)}, bf16[3,1,4,256,128]{4,3,2,1,0:T(8,128)(2,1)S(1)}, u32[]{:S(2)}, u32[]{:S(2)}) collective-permute-start(bf16[3,1,4,256,128]{4,3,2,1,0:T(8,128)(2,1)} %pad_maximum_fusion.1), channel_id=1, source_target_pairs={{0,1},{1,2},{2,3},{3,4},{4,5},{5,6},{6,7},{8,9},{9,10},{10,11},{11... | collective-permute-start | bytes 2359304 | tf_op jit(solution)/shard_map/ppermute | solution.py:16
  510.5 5.9 collective-permute-done.7
  517.3 6.4 scatter_fusion
  523.7 125.5 %all-reduce.3.cloned.1.call-done = (f32[27,128,128]{2,1,0:T(8,128)}, f32[8,128,128]{2,1,0:T(8,128)}) async-done(((f32[27,128,128]{2,1,0:T(8,128)}, f32[8,128,128]{2,1,0:T(8,128)}), (f32[27,128,128]{2,1,0:T(8,128)}, f32[8,128,128]{2,1,0:T(8,128)})) %all-reduce.3.cloned.1.call-update) | async-done | bytes 2293776 | tf_op jit(solution)/shard_map/psum | solution.py:161
  (503 shorter events, 376.3 us)
Async XLA Ops:
  7.2 11.2 %copy-start = (bf16[8,128,128]{2,1,0:T(8,128)(2,1)S(1)}, bf16[8,128,128]{2,1,0:T(8,128)(2,1)}, u32[]{:S(2)}) copy-start(bf16[8,128,128]{2,1,0:T(8,128)(2,1)} %param.13) | copy-start | bytes 786436
  7.2 11.0 %copy-start.16 = (s32[2048]{0:T(1024)S(1)}, s32[2048]{0:T(1024)}, u32[]{:S(2)}) copy-start(s32[2048]{0:T(1024)} %param.17) | copy-start | bytes 24580
  7.2 11.0 %copy-start.15 = (s32[27,2048]{1,0:T(8,128)S(1)}, s32[27,2048]{1,0:T(8,128)}, u32[]{:S(2)}) copy-start(s32[27,2048]{1,0:T(8,128)} %param.15) | copy-start | bytes 663556
  7.2 11.2 %copy-start.14 = (bf16[512,128]{1,0:T(8,128)(2,1)S(1)}, bf16[512,128]{1,0:T(8,128)(2,1)}, u32[]{:S(2)}) copy-start(bf16[512,128]{1,0:T(8,128)(2,1)} %param.14) | copy-start | bytes 393220
  7.2 642.0 %all-reduce.3.cloned.1.call-start = ((), (), s32[]{:S(2)}) async-start(), calls=%async_computation | async-start | bytes 4587520 | tf_op jit(solution)/shard_map/psum | solution.py:161
  12.0 11.4 %collective-permute-start = (bf16[1,1,4,256,128]{4,3,2,1,0:T(8,128)(2,1)S(1)}, bf16[1,1,4,256,128]{4,3,2,1,0:T(8,128)(2,1)S(1)}, u32[]{:S(2)}, u32[]{:S(2)}) collective-permute-start(bf16[1,1,4,256,128]{4,3,2,1,0:T(8,128)(2,1)S(1)} %bitcast.179), channel_id=1, source_target_pairs={{0,8},{8,16},{16,24},{1,9},{9,17},{17,25},{2,10},{10,18},{18,26},{... | collective-permute-start | bytes 786440 | tf_op jit(solution)/shard_map/ppermute | solution.py:16
  16.9 13.1 %collective-permute-start.1 = (bf16[1,1,4,256,128]{4,3,2,1,0:T(8,128)(2,1)S(1)}, bf16[1,1,4,256,128]{4,3,2,1,0:T(8,128)(2,1)S(1)}, u32[]{:S(2)}, u32[]{:S(2)}) collective-permute-start(bf16[1,1,4,256,128]{4,3,2,1,0:T(8,128)(2,1)S(1)} %bitcast.180), channel_id=1, source_target_pairs={{8,0},{16,8},{24,16},{9,1},{17,9},{25,17},{10,2},{18,10},{26,18},{... | collective-permute-start | bytes 786440 | tf_op jit(solution)/shard_map/ppermute | solution.py:17
  22.2 16.5 %copy-start.3 = (bf16[2048,128]{1,0:T(8,128)(2,1)S(1)}, bf16[2048,128]{1,0:T(8,128)(2,1)}, u32[]{:S(2)}) copy-start(bf16[2048,128]{1,0:T(8,128)(2,1)} %param.11) | copy-start | bytes 1572868
  30.1 6.9 %collective-permute-start.3 = (bf16[3,1,4,256,128]{4,3,2,1,0:T(8,128)(2,1)S(1)}, bf16[3,1,4,256,128]{4,3,2,1,0:T(8,128)(2,1)}, u32[]{:S(2)}, u32[]{:S(2)}) collective-permute-start(bf16[3,1,4,256,128]{4,3,2,1,0:T(8,128)(2,1)S(1)} %pad_maximum_fusion), channel_id=1, source_target_pairs={{1,0},{2,1},{3,2},{4,3},{5,4},{6,5},{7,6},{9,8},{10,9},{11,10},{12... | collective-permute-start | bytes 2359304 | tf_op jit(solution)/shard_map/ppermute | solution.py:17
  32.2 5.6 collective-permute-start.2
  39.6 130.2 %copy-start.10 = (bf16[16,128,128,1]{2,1,3,0:T(8,128)(2,1)S(1)}, bf16[16,128,128,1]{2,1,3,0:T(8,128)(2,1)}, u32[]{:S(2)}) copy-start(bf16[16,128,128,1]{2,1,3,0:T(8,128)(2,1)} %fusion.61) | copy-start | bytes 1572868
  481.7 7.4 %copy-start.11 = (bf16[2048,128]{1,0:T(8,128)(2,1)S(1)}, bf16[2048,128]{1,0:T(8,128)(2,1)}, u32[]{:S(2)}) copy-start(bf16[2048,128]{1,0:T(8,128)(2,1)} %get-tuple-element.227) | copy-start | bytes 1572868
  481.7 7.4 %copy-start.12 = (pred[16,32,128,8]{2,1,3,0:T(32,128)(4,1)S(1)}, pred[16,32,128,8]{2,1,3,0:T(32,128)(4,1)}, u32[]{:S(2)}) copy-start(pred[16,32,128,8]{2,1,3,0:T(32,128)(4,1)} %and_and_fusion) | copy-start | bytes 1572868
  484.4 7.3 %collective-permute-start.4 = (bf16[1,1,4,256,128]{4,3,2,1,0:T(8,128)(2,1)S(1)}, bf16[1,1,4,256,128]{4,3,2,1,0:T(8,128)(2,1)S(1)}, u32[]{:S(2)}, u32[]{:S(2)}) collective-permute-start(bf16[1,1,4,256,128]{4,3,2,1,0:T(8,128)(2,1)S(1)} %bitcast.168), channel_id=1, source_target_pairs={{0,8},{8,16},{16,24},{1,9},{9,17},{17,25},{2,10},{10,18},{18,26},{... | collective-permute-start | bytes 786440 | tf_op jit(solution)/shard_map/ppermute | solution.py:16
  487.8 8.3 %collective-permute-start.5 = (bf16[1,1,4,256,128]{4,3,2,1,0:T(8,128)(2,1)S(1)}, bf16[1,1,4,256,128]{4,3,2,1,0:T(8,128)(2,1)S(1)}, u32[]{:S(2)}, u32[]{:S(2)}) collective-permute-start(bf16[1,1,4,256,128]{4,3,2,1,0:T(8,128)(2,1)S(1)} %bitcast.169), channel_id=1, source_target_pairs={{8,0},{16,8},{24,16},{9,1},{17,9},{25,17},{10,2},{18,10},{26,18},{... | collective-permute-start | bytes 786440 | tf_op jit(solution)/shard_map/ppermute | solution.py:17
  489.6 17.1 %copy-start.8 = (bf16[16,32,8,128]{3,2,1,0:T(8,128)(2,1)}, bf16[16,32,8,128]{3,2,1,0:T(8,128)(2,1)S(1)}, u32[]{:S(2)}) copy-start(bf16[16,32,8,128]{3,2,1,0:T(8,128)(2,1)S(1)} %fusion.37) | copy-start | bytes 3145732
  491.7 4.4 copy-start.4
  496.1 1.0 copy-start.6
  497.1 11.0 %copy-start.17 = (s32[4,256]{1,0:T(4,128)S(1)}, s32[4,256]{1,0:T(4,128)}, u32[]{:S(2)}) copy-start(s32[4,256]{1,0:T(4,128)} %param.16) | copy-start | bytes 12292
  497.1 11.0 %copy-start.1 = (f32[25,128,128]{2,0,1:T(8,128)S(1)}, f32[25,128,128]{2,0,1:T(8,128)}, u32[]{:S(2)}) copy-start(f32[25,128,128]{2,0,1:T(8,128)} %get-tuple-element.117) | copy-start | bytes 4915204
  497.1 13.3 %collective-permute-start.6 = (bf16[3,1,4,256,128]{4,3,2,1,0:T(8,128)(2,1)}, bf16[3,1,4,256,128]{4,3,2,1,0:T(8,128)(2,1)S(1)}, u32[]{:S(2)}, u32[]{:S(2)}) collective-permute-start(bf16[3,1,4,256,128]{4,3,2,1,0:T(8,128)(2,1)} %pad_maximum_fusion.1), channel_id=1, source_target_pairs={{0,1},{1,2},{2,3},{3,4},{4,5},{5,6},{6,7},{8,9},{9,10},{10,11},{11... | collective-permute-start | bytes 2359304 | tf_op jit(solution)/shard_map/ppermute | solution.py:16
  505.3 11.1 %collective-permute-start.7 = (bf16[3,1,4,256,128]{4,3,2,1,0:T(8,128)(2,1)}, bf16[3,1,4,256,128]{4,3,2,1,0:T(8,128)(2,1)}, u32[]{:S(2)}, u32[]{:S(2)}) collective-permute-start(bf16[3,1,4,256,128]{4,3,2,1,0:T(8,128)(2,1)} %pad_maximum_fusion.1), channel_id=1, source_target_pairs={{1,0},{2,1},{3,2},{4,3},{5,4},{6,5},{7,6},{9,8},{10,9},{11,10},{12... | collective-permute-start | bytes 2359304 | tf_op jit(solution)/shard_map/ppermute | solution.py:17
  508.1 1.2 copy-start.9
  508.3 8.1 %copy-start.5 = (bf16[1,1,4,256,128]{4,3,2,1,0:T(8,128)(2,1)S(1)}, bf16[1,1,4,256,128]{4,3,2,1,0:T(8,128)(2,1)}, u32[]{:S(2)}) copy-start(bf16[1,1,4,256,128]{4,3,2,1,0:T(8,128)(2,1)} %copy-done.4) | copy-start | bytes 786436
  508.3 8.1 %copy-start.7 = (bf16[1,1,4,256,128]{4,3,2,1,0:T(8,128)(2,1)S(1)}, bf16[1,1,4,256,128]{4,3,2,1,0:T(8,128)(2,1)}, u32[]{:S(2)}) copy-start(bf16[1,1,4,256,128]{4,3,2,1,0:T(8,128)(2,1)} %copy-done.6) | copy-start | bytes 786436
  523.7 129.3 %copy-start.2 = (f32[2048,128]{1,0:T(8,128)}, f32[2048,128]{1,0:T(8,128)S(1)}, u32[]{:S(2)}) copy-start(f32[2048,128]{1,0:T(8,128)S(1)} %scatter_fusion) | copy-start | bytes 3145732
  649.3 2.9 copy-start.13
Sparse Core Ops, SparseCore 0:
  508.2 141.0 all-reduce.2
where the time goes:
time: 670 us; the launch traced here: 660 us
  matrix products  335 us (50%)
  waiting for transfers between devices  144 us (21%)
  local copies, waits for them, and re-layouts  123 us (18%)
  starting transfers between devices  25.8 us (4%)
  between operations  14.5 us (2%)
  other arithmetic  14.1 us (2%)
    psum x1, waiting for transfers between devices, body(): conv_grad, down_total = lax.psum((conv_part, down_part), ('slab', 'tile'))  126 us
    dot_general x27, matrix products, backward_step(): jnp.einsum('bn,bjc->njc', block_pick(src_block).astype(jnp.float32), with...  121 us
    dot_general x27, matrix products, backward_step(): jnp.einsum('bij,bic->bjc', row_pick(inner_one, valid_one).astype(jnp.floa...  59.4 us
    dot_general x27, matrix products, backward_step(): lax.dot_general(rows_one, pre_grad, (((0,), (0,)), ((), ())), preferred_e...  54.3 us
    eq x54, local copies, waits for them, and re-layouts, row_pick(): inner_one[:, :, None] == columns[None, None, :]  38.1 us
    and x54, local copies, waits for them, and re-layouts, row_pick(): (inner_one[:, :, None] == columns[None, None, :]) & valid_one[:, :, None]  36.8 us
    dot_general x27, matrix products, forward_step(): jnp.dot(rows_one, weight_one, preferred_element_type=jnp.float32)  31.6 us
    dot_general x27, matrix products, backward_step(): lax.dot_general(pre_grad, weight_one, (((1,), (1,)), ((), ())), preferred...  28.4 us
  transfers between devices with their start and end apart: 9, of which 5 were waited for; matrix products, arithmetic and copies ran while one was open for 3% of the time, Pallas kernels for 0%

commit v1 on v0

v1 whole, which is shorter than its diff:
```python
import jax
import jax.numpy as jnp
from jax import lax
from jax.experimental import pallas as pl
from jax.experimental.pallas import tpu as pltpu
from jax.sharding import PartitionSpec as P

BLOCK = 128
F32 = jnp.float32
BF16 = jnp.bfloat16
LAST = (((1,), (1,)), ((), ()))
FIRST = (((0,), (0,)), ((), ()))


def dot(a, b):
    return jnp.dot(a, b, preferred_element_type=F32)


def hot(rows, index):
    return (lax.broadcasted_iota(jnp.int32, (rows, index.shape[1]), 0) == index).astype(BF16)


def main_kernel(
    src, table, wflat, weight, down, cgrad, book, code,
    coarse, ext_grad, conv_grad, down_grad,
    gathered, pre_grad, spread, children,
):
    kernels, blocks = book.shape[0], book.shape[1]
    childs, _, quarter, chans = spread.shape
    live = blocks - 1
    ext_grad[...] = jnp.zeros_like(ext_grad)
    children[...] = jnp.zeros_like(children)
    for s in range(childs):
        one = lax.dot_general(cgrad[...], down[s], LAST, preferred_element_type=F32)
        spread[s] = one.astype(BF16).reshape(blocks, quarter, chans)

    def pick(k, b):
        return hot(BLOCK, book[k, pl.ds(b, 1), :] - src[k, b] * BLOCK)

    def forward(b, carry):
        for k in range(kernels):
            got = dot(table[src[k, b]], pick(k, b))
            gathered[k * BLOCK : (k + 1) * BLOCK, :] = got.astype(BF16)
        pre = dot(wflat[...], gathered[...]).T
        hidden = jnp.maximum(pre, 0.0).astype(BF16)
        own = code[pl.ds(b, 1), :]
        place = (own % childs) * quarter + (own // childs - b * quarter)
        place = jnp.where(own // childs < blocks * quarter, place, -1)
        family = hot(childs * quarter, place)
        kids = dot(family, hidden).astype(BF16)
        children[:, b] = kids.reshape(childs, quarter, chans)
        share = spread[:, b].reshape(childs * quarter, chans)
        back = lax.dot_general(family, share, FIRST, preferred_element_type=F32)
        pre_grad[b] = jnp.where(pre > 0, back, 0.0).astype(BF16)
        return carry

    lax.fori_loop(0, live, forward, 0)

    coarse_total = jnp.zeros(coarse.shape, F32)
    for s in range(childs):
        kids = children[s].reshape(blocks * quarter, chans)
        coarse_total += dot(kids, down[s])
        down_grad[s] = lax.dot_general(kids, cgrad[...], FIRST, preferred_element_type=F32)
    coarse[...] = coarse_total.astype(BF16)

    def backward(k, carry):
        total = jnp.zeros(conv_grad.shape[1:], F32)
        for b in range(0, live, 2):
            group = range(b, min(b + 2, live))
            sums = [dot(pick(k, i), pre_grad[i]).astype(BF16) for i in group]
            sums = jnp.concatenate(sums, axis=0)
            total += dot(jnp.concatenate([table[src[k, i]] for i in group], axis=1), sums)
            terms = lax.dot_general(sums, weight[k], LAST, preferred_element_type=F32)
            for place, i in enumerate(group):
                ext_grad[src[k, i]] += terms[place * BLOCK : (place + 1) * BLOCK]
        conv_grad[k] = total
        return carry

    lax.fori_loop(0, kernels, backward, 0)


def add_kernel(base, lists, coming, out):
    blocks = base.shape[0]
    for n in range(blocks):
        out[n] = base[n] + dot(hot(BLOCK, lists[...] - n * BLOCK), coming[...])


def body(features, conv_weight, down_weight, coarse_grad, rulebook, boundary_rows, parent_code):
    rows, chans = features.shape
    coarse_rows, out_chans = coarse_grad.shape
    list_len = boundary_rows.shape[1]
    childs = down_weight.shape[0]
    kernels = conv_weight.shape[0]
    blocks = rows // BLOCK
    halo_blocks = 4 * list_len // BLOCK
    total_blocks = blocks + halo_blocks

    def shift(value, axis, step):
        size = lax.axis_size(axis)
        pairs = [(i, i + step) for i in range(size) if 0 <= i + step < size]
        return lax.ppermute(value, axis, pairs)

    outgoing = features[boundary_rows]
    received = jnp.stack(
        [
            shift(outgoing[0], "slab", 1),
            shift(outgoing[1], "slab", -1),
            shift(outgoing[2], "tile", 1),
            shift(outgoing[3], "tile", -1),
        ]
    )
    extended = jnp.concatenate([features, received.reshape(4 * list_len, chans)], axis=0)
    table = extended.reshape(total_blocks, BLOCK, chans).transpose(0, 2, 1)
    wflat = conv_weight.transpose(2, 0, 1).reshape(out_chans, kernels * chans)
    book = rulebook.reshape(kernels, blocks, BLOCK)
    src = jnp.minimum(jnp.min(book, axis=2) // BLOCK, total_blocks - 1)
    vmem = pl.BlockSpec(memory_space=pltpu.VMEM)
    coarse, ext_grad, conv_part, down_part = pl.pallas_call(
        main_kernel,
        out_shape=(
            jax.ShapeDtypeStruct((coarse_rows, out_chans), BF16),
            jax.ShapeDtypeStruct((total_blocks, BLOCK, chans), F32),
            jax.ShapeDtypeStruct(conv_weight.shape, F32),
            jax.ShapeDtypeStruct(down_weight.shape, F32),
        ),
        in_specs=[pl.BlockSpec(memory_space=pltpu.SMEM)] + [vmem] * 7,
        out_specs=(vmem,) * 4,
        scratch_shapes=[
            pltpu.VMEM((kernels * BLOCK, BLOCK), BF16),
            pltpu.VMEM((blocks, BLOCK, chans), BF16),
            pltpu.VMEM((childs, blocks, coarse_rows // blocks, chans), BF16),
            pltpu.VMEM((childs, blocks, coarse_rows // blocks, chans), BF16),
        ],
        compiler_params=pltpu.CompilerParams(vmem_limit_bytes=40 * 2**20),
        name="sparse_conv",
    )(
        src, table, wflat, conv_weight, down_weight, coarse_grad, book,
        parent_code.reshape(blocks, BLOCK),
    )
    halo = ext_grad[blocks:].reshape(4, list_len, chans).astype(BF16)
    returned = jnp.concatenate(
        [
            shift(halo[0], "slab", -1),
            shift(halo[1], "slab", 1),
            shift(halo[2], "tile", -1),
            shift(halo[3], "tile", 1),
        ]
    )
    input_grad = pl.pallas_call(
        add_kernel,
        out_shape=jax.ShapeDtypeStruct((blocks, BLOCK, chans), F32),
        in_specs=[vmem] * 3,
        out_specs=vmem,
        compiler_params=pltpu.CompilerParams(vmem_limit_bytes=32 * 2**20),
        name="add_returned",
    )(ext_grad[:blocks], boundary_rows.reshape(1, 4 * list_len), returned)
    conv_grad, down_grad = lax.psum((conv_part, down_part), ("slab", "tile"))
    return (coarse, input_grad.reshape(rows, chans), conv_grad, down_grad)


def solution(mesh):
    return jax.shard_map(
        body,
        mesh=mesh,
        in_specs=(
            P(("slab", "tile"), None),
            P(),
            P(),
            P(("slab", "tile"), None),
            P(None, ("slab", "tile")),
            P(("slab", "tile"), None),
            P(("slab", "tile")),
        ),
        out_specs=(P(("slab", "tile"), None), P(("slab", "tile"), None), P(), P()),
        check_vma=False,
    )
```

time: 670 us -> 235 us (0.35); the launches traced: 660 us -> 234 us
  matrix products: 335 us -> 0 us
  local copies, waits for them, and re-layouts: 123 us -> 15.2 us
  Pallas kernels: 0 us -> 55.8 us
  waiting for transfers between devices: 144 us -> 125 us
  other arithmetic: 14.1 us -> 2.03 us
    dot_general x194 -> x0, matrix products: 335 us -> none  [the longest x27 121 us: backward_step(): jnp.einsum('bn,bjc->njc', block_pick(src_block).astype(jnp.float32), with...]
    pallas_call x0 -> x2, Pallas kernels: none -> 55.8 us  [the longest x1 53.6 us: body(): pl.pallas_call(main_kernel, out_shape=(jax.ShapeDtypeStruct((coarse_rows,...]
    eq x108 -> x0, local copies, waits for them, and re-layouts: 38.6 us -> none  [the longest x54 38.1 us: row_pick(): inner_one[:, :, None] == columns[None, None, :]]
    and x54 -> x0, local copies, waits for them, and re-layouts: 36.8 us -> none  [row_pick(): (inner_one[:, :, None] == columns[None, None, :]) & valid_one[:, :, None]]
    dynamic_update_slice x27 -> x0, local copies, waits for them, and re-layouts: 23 us -> none  [body(): lax.scan(forward_step, jnp.zeros((row_count, chan_count), jnp.float32), (...]
    ppermute x8, waiting for transfers between devices: 18.9 us -> 2.07 us  [shift(): return lax.ppermute(value, axis, pairs)]
    reshape x28 -> x2, local copies, waits for them, and re-layouts: 9.13 us -> 2.17 us  [the longest x1 1.17 us: body(): table = extended.reshape(total_blocks, BLOCK, chans).transpose(0, 2, 1)]
  transfers between devices with their start and end apart: 9 -> 9, of which waited for: 5 -> 3; matrix products, arithmetic and copies ran while one was open for 3% -> 1% of each run, Pallas kernels for 0% -> 1%
where the time goes in v1:
time: 235 us; the launch traced here: 234 us
  waiting for transfers between devices  125 us (53%)
  Pallas kernels  55.8 us (24%)
  starting transfers between devices  21.9 us (9%)
  local copies, waits for them, and re-layouts  15.2 us (6%)
  between operations  14.3 us (6%)
    psum x1, waiting for transfers between devices, body(): conv_grad, down_grad = lax.psum((conv_part, down_part), ('slab', 'tile'))  123 us
    pallas_call x1, Pallas kernels, body(): pl.pallas_call(main_kernel, out_shape=(jax.ShapeDtypeStruct((coarse_rows,...  53.6 us
    ppermute x8, starting transfers between devices, shift(): return lax.ppermute(value, axis, pairs)  21.8 us
    unnamed x29, local copies, waits for them, and re-layouts  8.84 us
  transfers between devices with their start and end apart: 9, of which 3 were waited for; matrix products, arithmetic and copies ran while one was open for 1% of the time, Pallas kernels for 1%

profile of v1, /device:TPU:0, one launch (start us, length us, event | category | flops | bytes accessed | tf_op | source)
XLA Modules:
  0.0 234.3 jit_solution(10733049271181000185)
XLA Ops:
  7.2 0.0 all-reduce.3.cloned.1.call-start
  7.2 0.7 fusion.3
  8.0 4.1 %gather_fusion = bf16[1024,128]{1,0:T(8,128)(2,1)S(1)} fusion(bf16[2048,128]{1,0:T(8,128)(2,1)} %param.7, s32[1024]{0:T(1024)S(1)} %broadcast_clamp_fusion), kind=kCustom, calls=%fused_computation | custom fusion | bytes 528384 | tf_op jit(solution)/shard_map/gather | solution.py:103
  12.1 4.8 %collective-permute-start = (bf16[256,128]{1,0:T(8,128)(2,1)S(1)}, bf16[256,128]{1,0:T(8,128)(2,1)S(1)}, u32[]{:S(2)}, u32[]{:S(2)}) collective-permute-start(bf16[256,128]{1,0:T(8,128)(2,1)S(1)} %get-tuple-element.20), channel_id=1, source_target_pairs={{0,8},{8,16},{16,24},{1,9},{9,17},{17,25},{2,10},{10,18},{18,26},{... | collective-permute-start | bytes 196616 | tf_op jit(solution)/shard_map/ppermute | solution.py:101
  16.9 1.3 collective-permute-start.1
  18.2 1.5 collective-permute-start.2
  19.7 1.3 collective-permute-start.3
  21.0 0.0 copy-start.8
  21.1 1.0 fusion.5
  22.1 1.0 copy.13.wflat
  23.2 1.3 collective-permute-done.3
  24.5 0.0 copy-start.7
  24.6 0.1 pad_maximum_fusion
  24.6 1.2 copy.12
  25.8 1.1 copy-done.1
  26.9 0.9 copy-done.3
  27.9 0.9 copy-done.5
  28.8 53.6 %sparse_conv.1 = (bf16[512,128]{1,0:T(8,128)(2,1)}, f32[24,128,128]{2,1,0:T(8,128)S(1)}, f32[27,128,128]{2,1,0:T(8,128)S(1)}, f32[8,128,128]{2,1,0:T(8,128)S(1)}) custom-call(s32[27,16]{1,0:T(8,128)S(1)} %fusion.1.src, bf16[24,128,128]{2,1,0:T(8,128)(2,1)S(1)} %bitcast.26, bf16[128,3456]{1,0:T(8,128)(2,1)S(1)} %copy.13.wflat, ...), custom_call_target="tpu_custom_call" | custom-call | tf_op jit(solution)/shard_map/sparse_conv/pallas_call | solution.py:118
  82.4 1.2 copy-done.2
  83.6 0.8 copy-done.4
  84.4 0.0 all-reduce.3.cloned.1.call-update
  84.4 0.1 convert.3
  84.6 1.3 collective-permute-start.4
  85.9 5.2 %collective-permute-start.5 = (bf16[256,128]{1,0:T(8,128)(2,1)S(1)}, bf16[256,128]{1,0:T(8,128)(2,1)S(1)}, u32[]{:S(2)}, u32[]{:S(2)}) collective-permute-start(bf16[256,128]{1,0:T(8,128)(2,1)S(1)} %bitcast.40), channel_id=1, source_target_pairs={{0,8},{8,16},{16,24},{1,9},{9,17},{17,25},{2,10},{10,18},{18,26},{... | collective-permute-start | bytes 196616 | tf_op jit(solution)/shard_map/ppermute | solution.py:101
  91.1 1.3 collective-permute-start.6
  92.4 5.2 %collective-permute-start.7 = (bf16[256,128]{1,0:T(8,128)(2,1)S(1)}, bf16[256,128]{1,0:T(8,128)(2,1)S(1)}, u32[]{:S(2)}, u32[]{:S(2)}) collective-permute-start(bf16[256,128]{1,0:T(8,128)(2,1)S(1)} %bitcast.36), channel_id=1, source_target_pairs={{0,1},{1,2},{2,3},{3,4},{4,5},{5,6},{6,7},{8,9},{9,10},{10,11},{11... | collective-permute-start | bytes 196616 | tf_op jit(solution)/shard_map/ppermute | solution.py:101
  97.6 0.1 slice.41.base
  97.7 0.7 collective-permute-done.7
  98.5 2.2 add_returned.1
  100.7 123.0 %all-reduce.3.cloned.1.call-done = (f32[27,128,128]{2,1,0:T(8,128)}, f32[8,128,128]{2,1,0:T(8,128)}) async-done(((f32[27,128,128]{2,1,0:T(8,128)}, f32[8,128,128]{2,1,0:T(8,128)}), (f32[27,128,128]{2,1,0:T(8,128)}, f32[8,128,128]{2,1,0:T(8,128)})) %all-reduce.3.cloned.1.call-update) | async-done | bytes 2293776 | tf_op jit(solution)/shard_map/psum | solution.py:157
  223.7 2.9 %copy.19 = f32[27,128,128]{2,1,0:T(8,128)} copy(f32[27,128,128]{2,1,0:T(8,128)} %get-tuple-element.26) | data formatting | bytes 3538944
  226.7 0.8 copy.20
  (32 shorter events, 0.2 us)
Async XLA Ops:
  7.2 13.8 %copy-start.10 = (s32[27,2048]{1,0:T(8,128)S(1)}, s32[27,2048]{1,0:T(8,128)}, u32[]{:S(2)}) copy-start(s32[27,2048]{1,0:T(8,128)} %param.11) | copy-start | bytes 663556
  7.2 216.5 %all-reduce.3.cloned.1.call-start = ((), (), s32[]{:S(2)}) async-start(), calls=%async_computation | async-start | bytes 4587520 | tf_op jit(solution)/shard_map/psum | solution.py:157
  8.0 14.2 %copy-start = (bf16[27,128,128]{2,1,0:T(8,128)(2,1)S(1)}, bf16[27,128,128]{2,1,0:T(8,128)(2,1)}, u32[]{:S(2)}) copy-start(bf16[27,128,128]{2,1,0:T(8,128)(2,1)} %weight.1) | copy-start | bytes 2654212
  12.1 11.1 %collective-permute-start = (bf16[256,128]{1,0:T(8,128)(2,1)S(1)}, bf16[256,128]{1,0:T(8,128)(2,1)S(1)}, u32[]{:S(2)}, u32[]{:S(2)}) collective-permute-start(bf16[256,128]{1,0:T(8,128)(2,1)S(1)} %get-tuple-element.20), channel_id=1, source_target_pairs={{0,8},{8,16},{16,24},{1,9},{9,17},{17,25},{2,10},{10,18},{18,26},{... | collective-permute-start | bytes 196616 | tf_op jit(solution)/shard_map/ppermute | solution.py:101
  16.9 6.2 %collective-permute-start.1 = (bf16[256,128]{1,0:T(8,128)(2,1)S(1)}, bf16[256,128]{1,0:T(8,128)(2,1)S(1)}, u32[]{:S(2)}, u32[]{:S(2)}) collective-permute-start(bf16[256,128]{1,0:T(8,128)(2,1)S(1)} %get-tuple-element.22), channel_id=1, source_target_pairs={{8,0},{16,8},{24,16},{9,1},{17,9},{25,17},{10,2},{18,10},{26,18},{... | collective-permute-start | bytes 196616 | tf_op jit(solution)/shard_map/ppermute | solution.py:101
  18.2 4.9 %collective-permute-start.2 = (bf16[256,128]{1,0:T(8,128)(2,1)S(1)}, bf16[256,128]{1,0:T(8,128)(2,1)S(1)}, u32[]{:S(2)}, u32[]{:S(2)}) collective-permute-start(bf16[256,128]{1,0:T(8,128)(2,1)S(1)} %get-tuple-element.21), channel_id=1, source_target_pairs={{0,1},{1,2},{2,3},{3,4},{4,5},{5,6},{6,7},{8,9},{9,10},{10,11},{11... | collective-permute-start | bytes 196616 | tf_op jit(solution)/shard_map/ppermute | solution.py:101
  19.7 4.8 %collective-permute-start.3 = (bf16[256,128]{1,0:T(8,128)(2,1)S(1)}, bf16[256,128]{1,0:T(8,128)(2,1)S(1)}, u32[]{:S(2)}, u32[]{:S(2)}) collective-permute-start(bf16[256,128]{1,0:T(8,128)(2,1)S(1)} %get-tuple-element.23), channel_id=1, source_target_pairs={{1,0},{2,1},{3,2},{4,3},{5,4},{6,5},{7,6},{9,8},{10,9},{11,10},{12... | collective-permute-start | bytes 196616 | tf_op jit(solution)/shard_map/ppermute | solution.py:101
  21.0 3.5 %copy-start.8 = (bf16[2048,128]{1,0:T(8,128)(2,1)S(1)}, bf16[2048,128]{1,0:T(8,128)(2,1)}, u32[]{:S(2)}) copy-start(bf16[2048,128]{1,0:T(8,128)(2,1)} %param.7) | copy-start | bytes 1572868
  24.5 1.3 copy-start.6
  24.5 1.2 copy-start.7
  25.8 1.1 copy-start.1
  26.9 0.9 copy-start.3
  27.9 0.9 copy-start.5
  82.4 1.2 copy-start.2
  83.6 0.8 copy-start.4
  84.4 13.2 %copy-start.11 = (s32[4,256]{1,0:T(4,128)S(1)}, s32[4,256]{1,0:T(4,128)}, u32[]{:S(2)}) copy-start(s32[4,256]{1,0:T(4,128)} %param.12) | copy-start | bytes 12292
  84.6 13.1 %collective-permute-start.4 = (bf16[256,128]{1,0:T(8,128)(2,1)S(1)}, bf16[256,128]{1,0:T(8,128)(2,1)S(1)}, u32[]{:S(2)}, u32[]{:S(2)}) collective-permute-start(bf16[256,128]{1,0:T(8,128)(2,1)S(1)} %bitcast.41), channel_id=1, source_target_pairs={{8,0},{16,8},{24,16},{9,1},{17,9},{25,17},{10,2},{18,10},{26,18},{... | collective-permute-start | bytes 196616 | tf_op jit(solution)/shard_map/ppermute | solution.py:101
  85.9 11.8 %collective-permute-start.5 = (bf16[256,128]{1,0:T(8,128)(2,1)S(1)}, bf16[256,128]{1,0:T(8,128)(2,1)S(1)}, u32[]{:S(2)}, u32[]{:S(2)}) collective-permute-start(bf16[256,128]{1,0:T(8,128)(2,1)S(1)} %bitcast.40), channel_id=1, source_target_pairs={{0,8},{8,16},{16,24},{1,9},{9,17},{17,25},{2,10},{10,18},{18,26},{... | collective-permute-start | bytes 196616 | tf_op jit(solution)/shard_map/ppermute | solution.py:101
  91.1 6.6 %collective-permute-start.6 = (bf16[256,128]{1,0:T(8,128)(2,1)S(1)}, bf16[256,128]{1,0:T(8,128)(2,1)S(1)}, u32[]{:S(2)}, u32[]{:S(2)}) collective-permute-start(bf16[256,128]{1,0:T(8,128)(2,1)S(1)} %bitcast.38), channel_id=1, source_target_pairs={{1,0},{2,1},{3,2},{4,3},{5,4},{6,5},{7,6},{9,8},{10,9},{11,10},{12... | collective-permute-start | bytes 196616 | tf_op jit(solution)/shard_map/ppermute | solution.py:101
  92.4 6.1 %collective-permute-start.7 = (bf16[256,128]{1,0:T(8,128)(2,1)S(1)}, bf16[256,128]{1,0:T(8,128)(2,1)S(1)}, u32[]{:S(2)}, u32[]{:S(2)}) collective-permute-start(bf16[256,128]{1,0:T(8,128)(2,1)S(1)} %bitcast.36), channel_id=1, source_target_pairs={{0,1},{1,2},{2,3},{3,4},{4,5},{5,6},{6,7},{8,9},{9,10},{10,11},{11... | collective-permute-start | bytes 196616 | tf_op jit(solution)/shard_map/ppermute | solution.py:101
  223.7 2.9 %copy-start.9 = (f32[8,128,128]{2,1,0:T(8,128)S(1)}, f32[8,128,128]{2,1,0:T(8,128)}, u32[]{:S(2)}) copy-start(f32[8,128,128]{2,1,0:T(8,128)} %get-tuple-element.27) | copy-start | bytes 1572868
Sparse Core Ops, SparseCore 0:
  84.5 139.1 all-reduce.2

commit v2 on v1

v2 whole, which is shorter than its diff:
```python
import functools

import jax
import jax.numpy as jnp
from jax import lax
from jax.experimental import pallas as pl
from jax.experimental.pallas import tpu as pltpu
from jax.sharding import PartitionSpec as P

BLOCK = 128
F32 = jnp.float32
BF16 = jnp.bfloat16
LAST = (((1,), (1,)), ((), ()))
FIRST = (((0,), (0,)), ((), ()))
MESH = pl.DeviceIdType.MESH


def dot(a, b):
    return jnp.dot(a, b, preferred_element_type=F32)


def hot(rows, index):
    return (lax.broadcasted_iota(jnp.int32, (rows, index.shape[1]), 0) == index).astype(BF16)


def main_kernel(
    src, table, wflat, weight, down, cgrad, book, code,
    coarse, part, local_grad, halo_grad,
    ext_grad, gathered, pre_grad, spread, children,
):
    kernels, blocks = book.shape[0], book.shape[1]
    childs, _, quarter, chans = spread.shape
    live = blocks - 1
    ext_grad[...] = jnp.zeros_like(ext_grad)
    children[...] = jnp.zeros_like(children)
    for s in range(childs):
        one = lax.dot_general(cgrad[...], down[s], LAST, preferred_element_type=F32)
        spread[s] = one.astype(BF16).reshape(blocks, quarter, chans)

    def pick(k, b):
        return hot(BLOCK, book[k, pl.ds(b, 1), :] - src[k, b] * BLOCK)

    def forward(b, carry):
        for k in range(kernels):
            got = dot(table[src[k, b]], pick(k, b))
            gathered[k * BLOCK : (k + 1) * BLOCK, :] = got.astype(BF16)
        pre = dot(wflat[...], gathered[...]).T
        hidden = jnp.maximum(pre, 0.0).astype(BF16)
        own = code[pl.ds(b, 1), :]
        place = (own % childs) * quarter + (own // childs - b * quarter)
        place = jnp.where(own // childs < blocks * quarter, place, -1)
        family = hot(childs * quarter, place)
        kids = dot(family, hidden).astype(BF16)
        children[:, b] = kids.reshape(childs, quarter, chans)
        share = spread[:, b].reshape(childs * quarter, chans)
        back = lax.dot_general(family, share, FIRST, preferred_element_type=F32)
        pre_grad[b] = jnp.where(pre > 0, back, 0.0).astype(BF16)
        return carry

    lax.fori_loop(0, live, forward, 0)

    coarse_total = jnp.zeros(coarse.shape, F32)
    for s in range(childs):
        kids = children[s].reshape(blocks * quarter, chans)
        coarse_total += dot(kids, down[s])
        one = lax.dot_general(kids, cgrad[...], FIRST, preferred_element_type=F32)
        part[(kernels + s) * BLOCK : (kernels + s + 1) * BLOCK, :] = one.astype(BF16)
    coarse[...] = coarse_total.astype(BF16)
    used = (kernels + childs) * BLOCK
    if used < part.shape[0]:
        part[used:, :] = jnp.zeros((part.shape[0] - used, part.shape[1]), BF16)

    def backward(k, carry):
        total = jnp.zeros(weight.shape[1:], F32)
        for b in range(0, live, 2):
            group = range(b, min(b + 2, live))
            sums = [dot(pick(k, i), pre_grad[i]).astype(BF16) for i in group]
            sums = jnp.concatenate(sums, axis=0)
            total += dot(jnp.concatenate([table[src[k, i]] for i in group], axis=1), sums)
            terms = lax.dot_general(sums, weight[k], LAST, preferred_element_type=F32)
            for place, i in enumerate(group):
                ext_grad[src[k, i]] += terms[place * BLOCK : (place + 1) * BLOCK]
        part[pl.ds(pl.multiple_of(k * BLOCK, BLOCK), BLOCK), :] = total.astype(BF16)
        return carry

    lax.fori_loop(0, kernels, backward, 0)
    local_grad[...] = ext_grad[:blocks]
    halo_grad[...] = ext_grad[blocks:].reshape(halo_grad.shape).astype(BF16)


def exchange(slab, tile, sems, base):
    me_s, me_t = lax.axis_index("slab"), lax.axis_index("tile")
    steps = ((1, 0), (-1, 0), (0, 1), (0, -1))

    def there(ds, dt):
        s, t = me_s + ds, me_t + dt
        return (s >= 0) & (s < slab) & (t >= 0) & (t < tile)

    def make(d, sign, src, dst):
        ds, dt = steps[d][0] * sign, steps[d][1] * sign
        to = (lax.rem(me_s + ds + slab, slab), lax.rem(me_t + dt + tile, tile))
        send, recv = sems
        return pltpu.make_async_remote_copy(
            src_ref=src, dst_ref=dst, send_sem=send.at[base + d], recv_sem=recv.at[base + d],
            device_id=to, device_id_type=MESH,
        )

    return steps, there, make


def greet_neighbours(slab, tile, barrier):
    me_s, me_t = lax.axis_index("slab"), lax.axis_index("tile")
    steps, there, _ = exchange(slab, tile, None, 0)
    for ds, dt in steps:

        @pl.when(there(ds, dt))
        def _(ds=ds, dt=dt):
            pl.semaphore_signal(
                barrier, inc=1, device_id=(me_s + ds, me_t + dt), device_id_type=MESH
            )


def neighbour_count(slab, tile):
    steps, there, _ = exchange(slab, tile, None, 0)
    return sum(jnp.where(there(ds, dt), 1, 0) for ds, dt in steps)


def send_all(slab, tile, sems, sign, src, dst):
    steps, there, make = exchange(slab, tile, sems, 0)
    for d, (ds, dt) in enumerate(steps):

        @pl.when(there(ds * sign, dt * sign))
        def _(d=d):
            make(d, sign, src.at[d], dst.at[d]).start()


def wait_all(slab, tile, sems, sign, src, dst):
    steps, there, make = exchange(slab, tile, sems, 0)
    for d, (ds, dt) in enumerate(steps):

        @pl.when(there(ds * sign, dt * sign))
        def _(d=d):
            make(d, sign, src.at[d], dst.at[d]).wait_send()

        @pl.when(there(-ds * sign, -dt * sign))
        def _(d=d):
            make(d, sign, src.at[d], dst.at[d]).wait_recv()


def halo_kernel(slab, tile, features, lists, table, outgoing, arrived, send, recv):
    blocks = features.shape[0]
    per_list = outgoing.shape[1]
    arrived[...] = jnp.zeros_like(arrived)
    barrier = pltpu.get_barrier_semaphore()
    greet_neighbours(slab, tile, barrier)
    for n in range(blocks):
        table[n] = features[n].astype(F32).T.astype(BF16)
    local = jnp.concatenate([table[n] for n in range(blocks)], axis=1)
    width = per_list * BLOCK
    for d in range(4):
        rows = hot(blocks * BLOCK, lists[:, d * width : (d + 1) * width])
        picked = dot(local, rows).astype(BF16)
        for j in range(per_list):
            outgoing[d, j] = picked[:, j * BLOCK : (j + 1) * BLOCK]
    pl.semaphore_wait(barrier, neighbour_count(slab, tile))
    send_all(slab, tile, (send, recv), 1, outgoing, arrived)
    wait_all(slab, tile, (send, recv), 1, outgoing, arrived)
    for d in range(4):
        for j in range(per_list):
            table[blocks + d * per_list + j] = arrived[d, j]


def reduce_kernel(
    slab, tile, part, halo, base, lists, total, grad,
    from_pair, after_pair, from_slab, after_slab, from_high, result, coming, send, recv,
):
    high_count = tile // 2
    chunk = part.shape[0] // (slab * tile)
    wide = high_count * chunk
    half = slab * wide
    me_s, me_t = lax.axis_index("slab"), lax.axis_index("tile")
    core, high = lax.rem(me_t, 2), lax.div(me_t, 2)
    pair = me_t + 1 - 2 * core

    def rows(start, count):
        return pl.ds(pl.multiple_of(start, 16), count)

    def remote(src, dst, i, s, t):
        return pltpu.make_async_remote_copy(
            src_ref=src, dst_ref=dst, send_sem=send.at[i], recv_sem=recv.at[i],
            device_id=(s, t), device_id_type=MESH,
        )

    slab_peers = [lax.rem(me_s + d, slab) for d in range(1, slab)]
    high_peers = [lax.rem(high + d, high_count) for d in range(1, high_count)]

    coming[...] = jnp.zeros_like(coming)
    barrier = pltpu.get_barrier_semaphore()
    greeted = [(me_s, pair)] + [(s, me_t) for s in slab_peers] + [(me_s, h * 2 + core) for h in high_peers]
    for to in greeted:
        pl.semaphore_signal(barrier, inc=1, device_id=to, device_id_type=MESH)
    beside = me_t + 2 * core - 1
    has_beside = (beside >= 0) & (beside < tile)

    @pl.when(has_beside)
    def _():
        pl.semaphore_signal(barrier, inc=1, device_id=(me_s, beside), device_id_type=MESH)

    pl.semaphore_wait(barrier, len(greeted) + jnp.where(has_beside, 1, 0))

    first = remote(part.at[rows((1 - core) * half, half)], from_pair, 4, me_s, pair)
    first.start()
    send_all(slab, tile, (send, recv), -1, halo, coming)
    first.wait()
    mine = part[rows(core * half, half), :].astype(F32) + from_pair[...].astype(F32)
    after_pair[...] = mine.astype(BF16)

    at = 5
    copies = []
    for d, s in enumerate(slab_peers):
        src = after_pair.at[rows(s * wide, wide)]
        copies.append(remote(src, from_slab.at[d], at + d, s, me_t))
        copies[-1].start()
    at += len(slab_peers)

    wait_all(slab, tile, (send, recv), -1, halo, coming)
    blocks = grad.shape[0]
    back = coming[...].reshape(-1, coming.shape[-1])
    for n in range(blocks):
        grad[n] = base[n] + dot(hot(BLOCK, lists[...] - n * BLOCK), back)

    for copy in copies:
        copy.wait()
    mine = after_pair[rows(me_s * wide, wide), :].astype(F32)
    for d in range(len(slab_peers)):
        mine += from_slab[d].astype(F32)
    after_slab[...] = mine.astype(BF16)

    copies = []
    for d, h in enumerate(high_peers):
        src = after_slab.at[rows(h * chunk, chunk)]
        copies.append(remote(src, from_high.at[d], at + d, me_s, h * 2 + core))
        copies[-1].start()
    at += len(high_peers)
    for copy in copies:
        copy.wait()
    mine = after_slab[rows(high * chunk, chunk), :].astype(F32)
    for d in range(len(high_peers)):
        mine += from_high[d].astype(F32)
    own = rows(((core * slab + me_s) * high_count + high) * chunk, chunk)
    result[own, :] = mine.astype(BF16)

    def share(where, peers, at):
        copies = [remote(result.at[where], result.at[where], at + d, s, t) for d, (s, t) in enumerate(peers)]
        for copy in copies:
            copy.start()
        for copy in copies:
            copy.wait()
        return at + len(peers)

    at = share(own, [(me_s, h * 2 + core) for h in high_peers], at)
    at = share(rows((core * slab + me_s) * wide, wide), [(s, me_t) for s in slab_peers], at)
    share(rows(core * half, half), [(me_s, pair)], at)
    total[...] = result[...]


def body(features, conv_weight, down_weight, coarse_grad, rulebook, boundary_rows, parent_code):
    rows, chans = features.shape
    coarse_rows, out_chans = coarse_grad.shape
    list_len = boundary_rows.shape[1]
    childs = down_weight.shape[0]
    kernels = conv_weight.shape[0]
    blocks = rows // BLOCK
    per_list = list_len // BLOCK
    total_blocks = blocks + 4 * per_list
    slab, tile = lax.axis_size("slab"), lax.axis_size("tile")
    high_count = tile // 2
    used = (kernels + childs) * BLOCK
    chunk = -(-used // (16 * slab * tile)) * 16
    vmem = pl.BlockSpec(memory_space=pltpu.VMEM)
    lists = boundary_rows.reshape(1, 4 * list_len)

    table = pl.pallas_call(
        functools.partial(halo_kernel, slab, tile),
        out_shape=jax.ShapeDtypeStruct((total_blocks, chans, BLOCK), BF16),
        in_specs=[vmem] * 2,
        out_specs=vmem,
        scratch_shapes=[
            pltpu.VMEM((4, per_list, chans, BLOCK), BF16),
            pltpu.VMEM((4, per_list, chans, BLOCK), BF16),
            pltpu.SemaphoreType.DMA((4,)),
            pltpu.SemaphoreType.DMA((4,)),
        ],
        compiler_params=pltpu.CompilerParams(
            collective_id=0, has_side_effects=True, vmem_limit_bytes=32 * 2**20
        ),
        name="halo",
    )(features.reshape(blocks, BLOCK, chans), lists)
    wflat = conv_weight.transpose(2, 0, 1).reshape(out_chans, kernels * chans)
    book = rulebook.reshape(kernels, blocks, BLOCK)
    src = jnp.minimum(jnp.min(book, axis=2) // BLOCK, total_blocks - 1)
    coarse, part, local_grad, halo_grad = pl.pallas_call(
        main_kernel,
        out_shape=(
            jax.ShapeDtypeStruct((coarse_rows, out_chans), BF16),
            jax.ShapeDtypeStruct((chunk * slab * tile, out_chans), BF16),
            jax.ShapeDtypeStruct((blocks, BLOCK, chans), F32),
            jax.ShapeDtypeStruct((4, list_len, chans), BF16),
        ),
        in_specs=[pl.BlockSpec(memory_space=pltpu.SMEM)] + [vmem] * 7,
        out_specs=(vmem,) * 4,
        scratch_shapes=[
            pltpu.VMEM((total_blocks, BLOCK, chans), F32),
            pltpu.VMEM((kernels * BLOCK, BLOCK), BF16),
            pltpu.VMEM((blocks, BLOCK, chans), BF16),
            pltpu.VMEM((childs, blocks, coarse_rows // blocks, chans), BF16),
            pltpu.VMEM((childs, blocks, coarse_rows // blocks, chans), BF16),
        ],
        compiler_params=pltpu.CompilerParams(vmem_limit_bytes=40 * 2**20),
        name="sparse_conv",
    )(
        src, table, wflat, conv_weight, down_weight, coarse_grad, book,
        parent_code.reshape(blocks, BLOCK),
    )
    wide = high_count * chunk
    copies = 4 + 2 * (1 + (slab - 1) + (high_count - 1))
    total, input_grad = pl.pallas_call(
        functools.partial(reduce_kernel, slab, tile),
        out_shape=(
            jax.ShapeDtypeStruct(part.shape, BF16),
            jax.ShapeDtypeStruct((blocks, BLOCK, chans), F32),
        ),
        in_specs=[vmem] * 4,
        out_specs=(vmem,) * 2,
        scratch_shapes=[
            pltpu.VMEM((slab * wide, out_chans), BF16),
            pltpu.VMEM((slab * wide, out_chans), BF16),
            pltpu.VMEM((slab - 1, wide, out_chans), BF16),
            pltpu.VMEM((wide, out_chans), BF16),
            pltpu.VMEM((high_count - 1, chunk, out_chans), BF16),
            pltpu.VMEM(part.shape, BF16),
            pltpu.VMEM((4, list_len, chans), BF16),
            pltpu.SemaphoreType.DMA((copies,)),
            pltpu.SemaphoreType.DMA((copies,)),
        ],
        compiler_params=pltpu.CompilerParams(
            collective_id=1, has_side_effects=True, vmem_limit_bytes=32 * 2**20
        ),
        name="reduce",
    )(part, halo_grad, local_grad, lists)
    total = total.astype(F32)
    conv_grad = total[: kernels * BLOCK].reshape(conv_weight.shape)
    down_grad = total[kernels * BLOCK : used].reshape(down_weight.shape)
    return (coarse, input_grad.reshape(rows, chans), conv_grad, down_grad)


def solution(mesh):
    return jax.shard_map(
        body,
        mesh=mesh,
        in_specs=(
            P(("slab", "tile"), None),
            P(),
            P(),
            P(("slab", "tile"), None),
            P(None, ("slab", "tile")),
            P(("slab", "tile"), None),
            P(("slab", "tile")),
        ),
        out_specs=(P(("slab", "tile"), None), P(("slab", "tile"), None), P(), P()),
        check_vma=False,
    )
```

time: 235 us -> 102 us (0.43)
  waiting for transfers between devices: 125 us -> 0 us
  Pallas kernels: 55.8 us -> 93.9 us
  starting transfers between devices: 21.9 us -> 0 us
  between operations: 14.3 us -> 0.74 us
  local copies, waits for them, and re-layouts: 15.2 us -> 6.95 us
    psum x1 -> x0, waiting for transfers between devices: 123 us -> none  [body(): conv_grad, down_grad = lax.psum((conv_part, down_part), ('slab', 'tile'))]
    pallas_call x1 -> x2, Pallas kernels: 2.22 us -> 40.1 us  [the longest x1 31.6 us: body(): pl.pallas_call(functools.partial(reduce_kernel, slab, tile), out_shape=(j...]
    ppermute x8 -> x0, starting transfers between devices: 21.8 us -> none  [shift(): return lax.ppermute(value, axis, pairs)]
    unnamed x29 -> x13, local copies, waits for them, and re-layouts: 8.84 us -> 3.8 us
    gather x1 -> x0, local copies, waits for them, and re-layouts: 4.07 us -> none  [body(): outgoing = features[boundary_rows]]
  transfers between devices with their start and end apart: 9 -> 0, of which waited for: 3 -> 0; matrix products, arithmetic and copies ran while one was open for 1% -> 0% of each run, Pallas kernels for 1% -> 0%
where the time goes in v2:
time: 102 us
  Pallas kernels  93.9 us (92%)
  local copies, waits for them, and re-layouts  6.95 us (7%)
    pallas_call x1, Pallas kernels, body(): pl.pallas_call(main_kernel, out_shape=(jax.ShapeDtypeStruct((coarse_rows,...  53.8 us
    pallas_call x1, Pallas kernels, body(): pl.pallas_call(functools.partial(reduce_kernel, slab, tile), out_shape=(j...  31.6 us
    pallas_call x1, Pallas kernels, body(): pl.pallas_call(functools.partial(halo_kernel, slab, tile), out_shape=jax....  8.44 us
    unnamed x13, local copies, waits for them, and re-layouts  3.8 us

profile of v2, /device:TPU:0, one launch (start us, length us, event | category | flops | bytes accessed | tf_op | source)
XLA Modules:
  0.0 102.1 jit_solution(17340407492807345828)
XLA Ops:
  0.6 0.0 copy-start
  0.6 0.8 copy.14
  1.4 1.0 copy.13
  2.4 0.5 fusion.3
  3.0 0.0 copy-start.1
  3.0 1.0 %copy-done.1 = bf16[2048,128]{1,0:T(8,128)(2,1)S(1)} copy-done((bf16[2048,128]{1,0:T(8,128)(2,1)S(1)}, bf16[2048,128]{1,0:T(8,128)(2,1)}, u32[]{:S(2)}) %copy-start.1) | copy-done | bytes 524312
  4.0 8.4 %halo.1.table = bf16[24,128,128]{2,1,0:T(8,128)(2,1)S(1)} custom-call(bf16[16,128,128]{2,1,0:T(8,128)(2,1)S(1)} %bitcast.16, s32[1,1024]{1,0:T(1,128)S(1)} %bitcast.17), custom_call_target="tpu_custom_call" | custom-call | tf_op jit(solution)/shard_map/halo/pallas_call | solution.py:283
  12.5 0.0 copy-done
  12.5 0.0 copy-start.2
  12.5 0.0 copy-start.3
  12.5 0.0 copy-start.4
  12.5 1.0 copy.12.wflat
  13.5 0.0 copy-done.2
  13.5 0.0 copy-done.3
  13.6 0.0 copy-done.4
  13.6 53.8 %sparse_conv.1 = (bf16[512,128]{1,0:T(8,128)(2,1)}, bf16[4608,128]{1,0:T(8,128)(2,1)S(1)}, f32[16,128,128]{2,1,0:T(8,128)S(1)}, bf16[4,256,128]{2,1,0:T(8,128)(2,1)S(1)}) custom-call(s32[27,16]{1,0:T(8,128)S(1)} %fusion.1.src, bf16[24,128,128]{2,1,0:T(8,128)(2,1)S(1)} %halo.1.table, bf16[128,3456]{1,0:T(8,128)(2,1)S(1)} %copy.12.wflat, ...), custom_call_target="tpu_custom_call" | custom-call | tf_op jit(solution)/shard_map/sparse_conv/pallas_call | solution.py:302
  67.4 31.6 %reduce.1 = (bf16[4608,128]{1,0:T(8,128)(2,1)S(1)}, f32[16,128,128]{2,1,0:T(8,128)S(1)}) custom-call(bf16[4608,128]{1,0:T(8,128)(2,1)S(1)} %get-tuple-element.11.part, bf16[4,256,128]{2,1,0:T(8,128)(2,1)S(1)} %get-tuple-element.12.halo, f32[16,128,128]{2,1,0:T(8,128)S(1)} %get-tuple-element.13.base, s32[1,1024]{1,0:T(1,128)S(1)} %bitcast.18), custom_call_target="tpu_custom_call" | custom-call | tf_op jit(solution)/shard_map/reduce/pallas_call | solution.py:327
  99.0 0.8 slice.9
  99.8 1.3 %slice.8 = f32[3456,128]{1,0:T(8,128)} slice(bf16[4608,128]{1,0:T(8,128)(2,1)S(1)} %get-tuple-element.15), slice={[0:3456], [0:128]} | slice | bytes 3538944 | tf_op jit(solution)/shard_map/slice | solution.py:352
  101.1 1.0 copy.16
  (1 shorter events, 0.0 us)
Async XLA Ops:
  0.6 11.8 %copy-start = (bf16[27,128,128]{2,1,0:T(8,128)(2,1)S(1)}, bf16[27,128,128]{2,1,0:T(8,128)(2,1)}, u32[]{:S(2)}) copy-start(bf16[27,128,128]{2,1,0:T(8,128)(2,1)} %weight.1) | copy-start | bytes 2654212
  3.0 1.0 %copy-start.1 = (bf16[2048,128]{1,0:T(8,128)(2,1)S(1)}, bf16[2048,128]{1,0:T(8,128)(2,1)}, u32[]{:S(2)}) copy-start(bf16[2048,128]{1,0:T(8,128)(2,1)} %param.7) | copy-start | bytes 1572868
  12.5 1.0 %copy-start.2 = (bf16[8,128,128]{2,1,0:T(8,128)(2,1)S(1)}, bf16[8,128,128]{2,1,0:T(8,128)(2,1)}, u32[]{:S(2)}) copy-start(bf16[8,128,128]{2,1,0:T(8,128)(2,1)} %down.1) | copy-start | bytes 786436
  12.5 1.0 %copy-start.3 = (bf16[512,128]{1,0:T(8,128)(2,1)S(1)}, bf16[512,128]{1,0:T(8,128)(2,1)}, u32[]{:S(2)}) copy-start(bf16[512,128]{1,0:T(8,128)(2,1)} %cgrad.1) | copy-start | bytes 393220
  12.5 1.0 %copy-start.4 = (s32[2048]{0:T(1024)S(1)}, s32[2048]{0:T(1024)}, u32[]{:S(2)}) copy-start(s32[2048]{0:T(1024)} %param.13) | copy-start | bytes 24580

commit v3 on v2

--- a/solution.py
+++ b/solution.py
@@ -8,6 +8,7 @@
 from jax.sharding import PartitionSpec as P
 
 BLOCK = 128
+GROUP = 3
 F32 = jnp.float32
 BF16 = jnp.bfloat16
 LAST = (((1,), (1,)), ((), ()))
@@ -20,17 +21,26 @@
 
 
 def hot(rows, index):
-    return (lax.broadcasted_iota(jnp.int32, (rows, index.shape[1]), 0) == index).astype(BF16)
+    short = jnp.clip(index, -1, rows).astype(jnp.int16)
+    same = lax.broadcasted_iota(jnp.int16, (rows, index.shape[1]), 0) == short
+    return jnp.where(same, jnp.ones((), BF16), jnp.zeros((), BF16))
+
+
+def diagonal(first, second):
+    empty = jnp.zeros_like(first)
+    top = jnp.concatenate([first, empty], axis=1)
+    return jnp.concatenate([top, jnp.concatenate([empty, second], axis=1)], axis=0)
 
 
 def main_kernel(
     src, table, wflat, weight, down, cgrad, book, code,
     coarse, part, local_grad, halo_grad,
-    ext_grad, gathered, pre_grad, spread, children,
+    ext_grad, gathered, pre_grad, sums, spread, children,
 ):
     kernels, blocks = book.shape[0], book.shape[1]
     childs, _, quarter, chans = spread.shape
-    live = blocks - 1
+    pairs = blocks // 2
+    group = sums.shape[0]
     ext_grad[...] = jnp.zeros_like(ext_grad)
     children[...] = jnp.zeros_like(children)
     for s in range(childs):
@@ -40,24 +50,32 @@
     def pick(k, b):
         return hot(BLOCK, book[k, pl.ds(b, 1), :] - src[k, b] * BLOCK)
 
-    def forward(b, carry):
+    def pair_of(k, p):
+        return jnp.concatenate([table[src[k, 2 * p]], table[src[k, 2 * p + 1]]], axis=1)
+
+    def forward(p, carry):
         for k in range(kernels):
-            got = dot(table[src[k, b]], pick(k, b))
+            got = dot(pair_of(k, p), diagonal(pick(k, 2 * p), pick(k, 2 * p + 1)))
             gathered[k * BLOCK : (k + 1) * BLOCK, :] = got.astype(BF16)
-        pre = dot(wflat[...], gathered[...]).T
-        hidden = jnp.maximum(pre, 0.0).astype(BF16)
-        own = code[pl.ds(b, 1), :]
-        place = (own % childs) * quarter + (own // childs - b * quarter)
-        place = jnp.where(own // childs < blocks * quarter, place, -1)
-        family = hot(childs * quarter, place)
-        kids = dot(family, hidden).astype(BF16)
-        children[:, b] = kids.reshape(childs, quarter, chans)
-        share = spread[:, b].reshape(childs * quarter, chans)
-        back = lax.dot_general(family, share, FIRST, preferred_element_type=F32)
-        pre_grad[b] = jnp.where(pre > 0, back, 0.0).astype(BF16)
+        pre_both = dot(wflat[...], gathered[...])
+        grads = []
+        for i in range(2):
+            b = 2 * p + i
+            pre = pre_both[:, i * BLOCK : (i + 1) * BLOCK].T
+            hidden = jnp.maximum(pre, 0.0).astype(BF16)
+            own = code[pl.ds(b, 1), :]
+            place = (own % childs) * quarter + (own // childs - b * quarter)
+            place = jnp.where(own // childs < blocks * quarter, place, -1)
+            family = hot(childs * quarter, place)
+            kids = dot(family, hidden).astype(BF16)
+            children[:, b] = kids.reshape(childs, quarter, chans)
+            share = spread[:, b].reshape(childs * quarter, chans)
+            back = lax.dot_general(family, share, FIRST, preferred_element_type=F32)
+            grads.append(jnp.where(pre > 0, back, 0.0).astype(BF16))
+        pre_grad[p] = diagonal(*grads)
         return carry
 
-    lax.fori_loop(0, live, forward, 0)
+    lax.fori_loop(0, pairs, forward, 0)
 
     coarse_total = jnp.zeros(coarse.shape, F32)
     for s in range(childs):
@@ -70,20 +88,31 @@
     if used < part.shape[0]:
         part[used:, :] = jnp.zeros((part.shape[0] - used, part.shape[1]), BF16)
 
-    def backward(k, carry):
-        total = jnp.zeros(weight.shape[1:], F32)
-        for b in range(0, live, 2):
-            group = range(b, min(b + 2, live))
-            sums = [dot(pick(k, i), pre_grad[i]).astype(BF16) for i in group]
-            sums = jnp.concatenate(sums, axis=0)
-            total += dot(jnp.concatenate([table[src[k, i]] for i in group], axis=1), sums)
-            terms = lax.dot_general(sums, weight[k], LAST, preferred_element_type=F32)
-            for place, i in enumerate(group):
-                ext_grad[src[k, i]] += terms[place * BLOCK : (place + 1) * BLOCK]
-        part[pl.ds(pl.multiple_of(k * BLOCK, BLOCK), BLOCK), :] = total.astype(BF16)
+    def backward(step, carry):
+        first = step * group
+        for p in range(pairs):
+            picks = [
+                jnp.concatenate([pick(first + g, 2 * p), pick(first + g, 2 * p + 1)], axis=1)
+                for g in range(group)
+            ]
+            both = dot(jnp.concatenate(picks, axis=0), pre_grad[p]).astype(BF16)
+            for g in range(group):
+                sums[g, p] = both[g * BLOCK : (g + 1) * BLOCK]
+        for g in range(group):
+            k = first + g
+            twice = diagonal(weight[k], weight[k])
+            total = jnp.zeros(weight.shape[1:], F32)
+            for p in range(pairs):
+                both = sums[g, p]
+                terms = lax.dot_general(both, twice, LAST, preferred_element_type=F32)
+                stacked = jnp.concatenate([both[:, :BLOCK], both[:, BLOCK:]], axis=0)
+                total += dot(pair_of(k, p), stacked)
+                for i in range(2):
+                    ext_grad[src[k, 2 * p + i]] += terms[:, i * BLOCK : (i + 1) * BLOCK]
+            part[pl.ds(pl.multiple_of(k * BLOCK, BLOCK), BLOCK), :] = total.astype(BF16)
         return carry
 
-    lax.fori_loop(0, kernels, backward, 0)
+    lax.fori_loop(0, kernels // group, backward, 0)
     local_grad[...] = ext_grad[:blocks]
     halo_grad[...] = ext_grad[blocks:].reshape(halo_grad.shape).astype(BF16)
 
@@ -311,8 +340,9 @@
         out_specs=(vmem,) * 4,
         scratch_shapes=[
             pltpu.VMEM((total_blocks, BLOCK, chans), F32),
-            pltpu.VMEM((kernels * BLOCK, BLOCK), BF16),
-            pltpu.VMEM((blocks, BLOCK, chans), BF16),
+            pltpu.VMEM((kernels * BLOCK, 2 * BLOCK), BF16),
+            pltpu.VMEM((blocks // 2, 2 * BLOCK, 2 * chans), BF16),
+            pltpu.VMEM((GROUP, blocks // 2, BLOCK, 2 * chans), BF16),
             pltpu.VMEM((childs, blocks, coarse_rows // blocks, chans), BF16),
             pltpu.VMEM((childs, blocks, coarse_rows // blocks, chans), BF16),
         ],

time: 102 us -> 78.5 us (0.77)
  Pallas kernels: 93.9 us -> 69.7 us
    pallas_call x1, Pallas kernels: 53.8 us -> 29.7 us  [body(): pl.pallas_call(main_kernel, out_shape=(jax.ShapeDtypeStruct((coarse_rows,...]
where the time goes in v3:
time: 78.5 us; the launch traced here: 78 us
  Pallas kernels  69.7 us (89%)
  local copies, waits for them, and re-layouts  6.95 us (9%)
    pallas_call x1, Pallas kernels, body(): pl.pallas_call(functools.partial(reduce_kernel, slab, tile), out_shape=(j...  31.5 us
    pallas_call x1, Pallas kernels, body(): pl.pallas_call(main_kernel, out_shape=(jax.ShapeDtypeStruct((coarse_rows,...  29.7 us
    pallas_call x1, Pallas kernels, body(): pl.pallas_call(functools.partial(halo_kernel, slab, tile), out_shape=jax....  8.44 us
    unnamed x13, local copies, waits for them, and re-layouts  3.8 us

profile of v3, /device:TPU:0, one launch (start us, length us, event | category | flops | bytes accessed | tf_op | source)
XLA Modules:
  0.0 78.0 jit_solution(9678510582479061598)
XLA Ops:
  0.6 0.0 copy-start
  0.6 0.8 copy.14
  1.4 1.0 %copy.13 = s32[4,8,16,128]{3,2,1,0:T(8,128)S(1)} copy(s32[4,8,16,128]{3,1,2,0:T(8,128)} %bitcast.23) | data formatting | bytes 524288
  2.4 0.5 fusion.3
  3.0 0.0 copy-start.1
  3.0 1.0 %copy-done.1 = bf16[2048,128]{1,0:T(8,128)(2,1)S(1)} copy-done((bf16[2048,128]{1,0:T(8,128)(2,1)S(1)}, bf16[2048,128]{1,0:T(8,128)(2,1)}, u32[]{:S(2)}) %copy-start.1) | copy-done | bytes 524312
  4.0 8.4 %halo.1.table = bf16[24,128,128]{2,1,0:T(8,128)(2,1)S(1)} custom-call(bf16[16,128,128]{2,1,0:T(8,128)(2,1)S(1)} %bitcast.16, s32[1,1024]{1,0:T(1,128)S(1)} %bitcast.17), custom_call_target="tpu_custom_call" | custom-call | tf_op jit(solution)/shard_map/halo/pallas_call | solution.py:312
  12.5 0.0 copy-done
  12.5 0.0 copy-start.2
  12.5 0.0 copy-start.3
  12.5 0.0 copy-start.4
  12.5 1.0 %copy.12.wflat = bf16[128,3456]{1,0:T(8,128)(2,1)S(1)} copy(bf16[128,3456]{0,1:T(8,128)(2,1)S(1)} %bitcast.14) | data formatting | bytes 1769472 | tf_op jit(solution)/shard_map/reshape | solution.py:328
  13.5 0.0 copy-done.2
  13.5 0.0 copy-done.3
  13.6 0.0 copy-done.4
  13.6 29.7 %sparse_conv.1 = (bf16[512,128]{1,0:T(8,128)(2,1)}, bf16[4608,128]{1,0:T(8,128)(2,1)S(1)}, f32[16,128,128]{2,1,0:T(8,128)S(1)}, bf16[4,256,128]{2,1,0:T(8,128)(2,1)S(1)}) custom-call(s32[27,16]{1,0:T(8,128)S(1)} %fusion.1.src, bf16[24,128,128]{2,1,0:T(8,128)(2,1)S(1)} %halo.1.table, bf16[128,3456]{1,0:T(8,128)(2,1)S(1)} %copy.12.wflat, ...), custom_call_target="tpu_custom_call" | custom-call | tf_op jit(solution)/shard_map/sparse_conv/pallas_call | solution.py:331
  43.3 31.5 %reduce.1 = (bf16[4608,128]{1,0:T(8,128)(2,1)S(1)}, f32[16,128,128]{2,1,0:T(8,128)S(1)}) custom-call(bf16[4608,128]{1,0:T(8,128)(2,1)S(1)} %get-tuple-element.11.part, bf16[4,256,128]{2,1,0:T(8,128)(2,1)S(1)} %get-tuple-element.12.halo, f32[16,128,128]{2,1,0:T(8,128)S(1)} %get-tuple-element.13.base, s32[1,1024]{1,0:T(1,128)S(1)} %bitcast.18), custom_call_target="tpu_custom_call" | custom-call | tf_op jit(solution)/shard_map/reduce/pallas_call | solution.py:357
  74.8 0.8 %slice.9 = f32[1024,128]{1,0:T(8,128)} slice(bf16[4608,128]{1,0:T(8,128)(2,1)S(1)} %get-tuple-element.15), slice={[3456:4480], [0:128]} | slice | bytes 1048576 | tf_op jit(solution)/shard_map/slice | solution.py:383
  75.7 1.3 %slice.8 = f32[3456,128]{1,0:T(8,128)} slice(bf16[4608,128]{1,0:T(8,128)(2,1)S(1)} %get-tuple-element.15), slice={[0:3456], [0:128]} | slice | bytes 3538944 | tf_op jit(solution)/shard_map/slice | solution.py:382
  77.0 1.0 %copy.16 = f32[2048,128]{1,0:T(8,128)} copy(f32[2048,128]{1,0:T(8,128)S(1)} %bitcast.15) | data formatting | bytes 2097152
  (1 shorter events, 0.0 us)
Async XLA Ops:
  0.6 11.8 %copy-start = (bf16[27,128,128]{2,1,0:T(8,128)(2,1)S(1)}, bf16[27,128,128]{2,1,0:T(8,128)(2,1)}, u32[]{:S(2)}) copy-start(bf16[27,128,128]{2,1,0:T(8,128)(2,1)} %weight.1) | copy-start | bytes 2654212
  3.0 1.0 %copy-start.1 = (bf16[2048,128]{1,0:T(8,128)(2,1)S(1)}, bf16[2048,128]{1,0:T(8,128)(2,1)}, u32[]{:S(2)}) copy-start(bf16[2048,128]{1,0:T(8,128)(2,1)} %param.7) | copy-start | bytes 1572868
  12.5 1.0 %copy-start.2 = (bf16[8,128,128]{2,1,0:T(8,128)(2,1)S(1)}, bf16[8,128,128]{2,1,0:T(8,128)(2,1)}, u32[]{:S(2)}) copy-start(bf16[8,128,128]{2,1,0:T(8,128)(2,1)} %down.1) | copy-start | bytes 786436
  12.5 1.0 %copy-start.3 = (bf16[512,128]{1,0:T(8,128)(2,1)S(1)}, bf16[512,128]{1,0:T(8,128)(2,1)}, u32[]{:S(2)}) copy-start(bf16[512,128]{1,0:T(8,128)(2,1)} %cgrad.1) | copy-start | bytes 393220
  12.5 1.0 %copy-start.4 = (s32[2048]{0:T(1024)S(1)}, s32[2048]{0:T(1024)}, u32[]{:S(2)}) copy-start(s32[2048]{0:T(1024)} %param.13) | copy-start | bytes 24580

commit v4 on v3

--- a/solution.py
+++ b/solution.py
@@ -199,14 +199,8 @@
             table[blocks + d * per_list + j] = arrived[d, j]
 
 
-def reduce_kernel(
-    slab, tile, part, halo, base, lists, total, grad,
-    from_pair, after_pair, from_slab, after_slab, from_high, result, coming, send, recv,
-):
+def reduce_kernel(slab, tile, pieces, part, halo, base, lists, total, grad, result, coming, send, recv, *buffers):
     high_count = tile // 2
-    chunk = part.shape[0] // (slab * tile)
-    wide = high_count * chunk
-    half = slab * wide
     me_s, me_t = lax.axis_index("slab"), lax.axis_index("tile")
     core, high = lax.rem(me_t, 2), lax.div(me_t, 2)
     pair = me_t + 1 - 2 * core
@@ -214,18 +208,80 @@
     def rows(start, count):
         return pl.ds(pl.multiple_of(start, 16), count)
 
-    def remote(src, dst, i, s, t):
+    def remote(src, dst, i, to):
         return pltpu.make_async_remote_copy(
             src_ref=src, dst_ref=dst, send_sem=send.at[i], recv_sem=recv.at[i],
-            device_id=(s, t), device_id_type=MESH,
+            device_id=to, device_id_type=MESH,
         )
 
     slab_peers = [lax.rem(me_s + d, slab) for d in range(1, slab)]
     high_peers = [lax.rem(high + d, high_count) for d in range(1, high_count)]
+    along_slab = (slab, me_s, [(s, (s, me_t)) for s in slab_peers])
+    along_high = (high_count, high, [(h, (me_s, h * 2 + core)) for h in high_peers])
+    one_way = 1 + len(slab_peers) + len(high_peers)
+
+    def flow(start, piece, outer, inner, at, from_pair, after_pair, from_outer, after_outer, from_inner):
+        outer_count, outer_me, outer_peers = outer
+        inner_count, inner_me, inner_peers = inner
+        wide = inner_count * piece
+        half = outer_count * wide
+
+        def scatter(held, size, landing, peers, at):
+            copies = []
+            for d, (index, to) in enumerate(peers):
+                copies.append(remote(held.at[rows(index * size, size)], landing.at[d], at + d, to))
+                copies[-1].start()
+            return copies
+
+        def share(first_row, count, devices, at):
+            where = rows(first_row, count)
+            copies = [remote(result.at[where], result.at[where], at + d, to) for d, to in enumerate(devices)]
+            for copy in copies:
+                copy.start()
+            return copies
+
+        def wait(copies):
+            for copy in copies:
+                copy.wait()
+
+        def summed(held, size, me, landing, peers):
+            mine = held[rows(me * size, size), :].astype(F32)
+            for d in range(len(peers)):
+                mine += landing[d].astype(F32)
+            return mine.astype(BF16)
+
+        first = remote(part.at[rows(start + (1 - core) * half, half)], from_pair, at, (me_s, pair))
+        first.start()
+        yield
+        first.wait()
+        mine = part[rows(start + core * half, half), :].astype(F32) + from_pair[...].astype(F32)
+        after_pair[...] = mine.astype(BF16)
+        copies = scatter(after_pair, wide, from_outer, outer_peers, at + 1)
+        yield
+        wait(copies)
+        after_outer[...] = summed(after_pair, wide, outer_me, from_outer, outer_peers)
+        copies = scatter(after_outer, piece, from_inner, inner_peers, at + 1 + len(outer_peers))
+        yield
+        wait(copies)
+        own_half = start + core * half
+        own_wide = own_half + outer_me * wide
+        own = own_wide + inner_me * piece
+        result[rows(own, piece), :] = summed(after_outer, piece, inner_me, from_inner, inner_peers)
+        at += one_way
+        copies = share(own, piece, [to for _, to in inner_peers], at)
+        yield
+        wait(copies)
+        copies = share(own_wide, wide, [to for _, to in outer_peers], at + len(inner_peers))
+        yield
+        wait(copies)
+        copies = share(own_half, half, [(me_s, pair)], at + one_way - 1)
+        yield
+        wait(copies)
+        yield
 
     coming[...] = jnp.zeros_like(coming)
     barrier = pltpu.get_barrier_semaphore()
-    greeted = [(me_s, pair)] + [(s, me_t) for s in slab_peers] + [(me_s, h * 2 + core) for h in high_peers]
+    greeted = [(me_s, pair)] + [to for _, to in along_slab[2]] + [to for _, to in along_high[2]]
     for to in greeted:
         pl.semaphore_signal(barrier, inc=1, device_id=to, device_id_type=MESH)
     beside = me_t + 2 * core - 1
@@ -237,59 +293,22 @@
 
     pl.semaphore_wait(barrier, len(greeted) + jnp.where(has_beside, 1, 0))
 
-    first = remote(part.at[rows((1 - core) * half, half)], from_pair, 4, me_s, pair)
-    first.start()
-    send_all(slab, tile, (send, recv), -1, halo, coming)
-    first.wait()
-    mine = part[rows(core * half, half), :].astype(F32) + from_pair[...].astype(F32)
-    after_pair[...] = mine.astype(BF16)
-
-    at = 5
-    copies = []
-    for d, s in enumerate(slab_peers):
-        src = after_pair.at[rows(s * wide, wide)]
-        copies.append(remote(src, from_slab.at[d], at + d, s, me_t))
-        copies[-1].start()
-    at += len(slab_peers)
-
-    wait_all(slab, tile, (send, recv), -1, halo, coming)
-    blocks = grad.shape[0]
-    back = coming[...].reshape(-1, coming.shape[-1])
-    for n in range(blocks):
-        grad[n] = base[n] + dot(hot(BLOCK, lists[...] - n * BLOCK), back)
-
-    for copy in copies:
-        copy.wait()
-    mine = after_pair[rows(me_s * wide, wide), :].astype(F32)
-    for d in range(len(slab_peers)):
-        mine += from_slab[d].astype(F32)
-    after_slab[...] = mine.astype(BF16)
-
-    copies = []
-    for d, h in enumerate(high_peers):
-        src = after_slab.at[rows(h * chunk, chunk)]
-        copies.append(remote(src, from_high.at[d], at + d, me_s, h * 2 + core))
-        copies[-1].start()
-    at += len(high_peers)
-    for copy in copies:
-        copy.wait()
-    mine = after_slab[rows(high * chunk, chunk), :].astype(F32)
-    for d in range(len(high_peers)):
-        mine += from_high[d].astype(F32)
-    own = rows(((core * slab + me_s) * high_count + high) * chunk, chunk)
-    result[own, :] = mine.astype(BF16)
-
-    def share(where, peers, at):
-        copies = [remote(result.at[where], result.at[where], at + d, s, t) for d, (s, t) in enumerate(peers)]
-        for copy in copies:
-            copy.start()
-        for copy in copies:
-            copy.wait()
-        return at + len(peers)
-
-    at = share(own, [(me_s, h * 2 + core) for h in high_peers], at)
-    at = share(rows((core * slab + me_s) * wide, wide), [(s, me_t) for s in slab_peers], at)
-    share(rows(core * half, half), [(me_s, pair)], at)
+    count = len(buffers) // 2
+    flows = [
+        flow(0, pieces[0], along_slab, along_high, 4, *buffers[:count]),
+        flow(pieces[0] * slab * tile, pieces[1], along_high, along_slab, 4 + 2 * one_way, *buffers[count:]),
+    ]
+    for stage in range(7):
+        for one in flows:
+            next(one)
+        if stage == 0:
+            send_all(slab, tile, (send, recv), -1, halo, coming)
+        if stage == 1:
+            wait_all(slab, tile, (send, recv), -1, halo, coming)
+            blocks = grad.shape[0]
+            back = coming[...].reshape(-1, coming.shape[-1])
+            for n in range(blocks):
+                grad[n] = base[n] + dot(hot(BLOCK, lists[...] - n * BLOCK), back)
     total[...] = result[...]
 
 
@@ -352,10 +371,17 @@
         src, table, wflat, conv_weight, down_weight, coarse_grad, book,
         parent_code.reshape(blocks, BLOCK),
     )
-    wide = high_count * chunk
-    copies = 4 + 2 * (1 + (slab - 1) + (high_count - 1))
+
+    def landings(piece, outer, inner):
+        wide = inner * piece
+        shapes = [(outer * wide,), (outer * wide,), (outer - 1, wide), (wide,), (inner - 1, piece)]
+        return [pltpu.VMEM(shape + (out_chans,), BF16) for shape in shapes]
+
+    first_piece = -(-chunk * 2 // 48) * 16
+    pieces = (first_piece, chunk - first_piece)
+    copies = 4 + 4 * (1 + (slab - 1) + (high_count - 1))
     total, input_grad = pl.pallas_call(
-        functools.partial(reduce_kernel, slab, tile),
+        functools.partial(reduce_kernel, slab, tile, pieces),
         out_shape=(
             jax.ShapeDtypeStruct(part.shape, BF16),
             jax.ShapeDtypeStruct((blocks, BLOCK, chans), F32),
@@ -363,16 +389,13 @@
         in_specs=[vmem] * 4,
         out_specs=(vmem,) * 2,
         scratch_shapes=[
-            pltpu.VMEM((slab * wide, out_chans), BF16),
-            pltpu.VMEM((slab * wide, out_chans), BF16),
-            pltpu.VMEM((slab - 1, wide, out_chans), BF16),
-            pltpu.VMEM((wide, out_chans), BF16),
-            pltpu.VMEM((high_count - 1, chunk, out_chans), BF16),
             pltpu.VMEM(part.shape, BF16),
             pltpu.VMEM((4, list_len, chans), BF16),
             pltpu.SemaphoreType.DMA((copies,)),
             pltpu.SemaphoreType.DMA((copies,)),
-        ],
+        ]
+        + landings(pieces[0], slab, high_count)
+        + landings(pieces[1], high_count, slab),
         compiler_params=pltpu.CompilerParams(
             collective_id=1, has_side_effects=True, vmem_limit_bytes=32 * 2**20
         ),

time: 78.5 us -> 73.5 us (0.936)
  Pallas kernels: 69.7 us -> 65 us
    pallas_call x1, Pallas kernels: 31.5 us -> 26.8 us  [body(): pl.pallas_call(functools.partial(reduce_kernel, slab, tile, pieces), out_...]
where the time goes in v4:
time: 73.5 us; the launch traced here: 73.3 us
  Pallas kernels  65 us (88%)
  local copies, waits for them, and re-layouts  6.95 us (9%)
  between operations  0.74 us (1%)
    pallas_call x1, Pallas kernels, body(): pl.pallas_call(main_kernel, out_shape=(jax.ShapeDtypeStruct((coarse_rows,...  29.7 us
    pallas_call x1, Pallas kernels, body(): pl.pallas_call(functools.partial(reduce_kernel, slab, tile, pieces), out_...  26.8 us
    pallas_call x1, Pallas kernels, body(): pl.pallas_call(functools.partial(halo_kernel, slab, tile), out_shape=jax....  8.44 us
    unnamed x13, local copies, waits for them, and re-layouts  3.8 us

profile of v4, /device:TPU:0, one launch (start us, length us, event | category | flops | bytes accessed | tf_op | source)
XLA Modules:
  0.0 73.3 jit_solution(9887216575544525514)
XLA Ops:
  0.6 0.0 copy-start
  0.6 0.8 %copy.14 = s32[1,1,4,256]{3,1,2,0:T(1,128)S(1)} copy(s32[1,1,4,256]{3,2,1,0:T(4,128)} %bitcast.24) | data formatting | bytes 8192
  1.4 1.0 %copy.13 = s32[4,8,16,128]{3,2,1,0:T(8,128)S(1)} copy(s32[4,8,16,128]{3,1,2,0:T(8,128)} %bitcast.23) | data formatting | bytes 524288
  2.4 0.5 fusion.3
  3.0 0.0 copy-start.1
  3.0 1.0 %copy-done.1 = bf16[2048,128]{1,0:T(8,128)(2,1)S(1)} copy-done((bf16[2048,128]{1,0:T(8,128)(2,1)S(1)}, bf16[2048,128]{1,0:T(8,128)(2,1)}, u32[]{:S(2)}) %copy-start.1) | copy-done | bytes 524312
  4.0 8.4 %halo.1.table = bf16[24,128,128]{2,1,0:T(8,128)(2,1)S(1)} custom-call(bf16[16,128,128]{2,1,0:T(8,128)(2,1)S(1)} %bitcast.16, s32[1,1024]{1,0:T(1,128)S(1)} %bitcast.17), custom_call_target="tpu_custom_call" | custom-call | tf_op jit(solution)/shard_map/halo/pallas_call | solution.py:331
  12.5 0.0 copy-done
  12.5 0.0 copy-start.2
  12.5 0.0 copy-start.3
  12.5 0.0 copy-start.4
  12.5 1.0 %copy.12.wflat = bf16[128,3456]{1,0:T(8,128)(2,1)S(1)} copy(bf16[128,3456]{0,1:T(8,128)(2,1)S(1)} %bitcast.14) | data formatting | bytes 1769472 | tf_op jit(solution)/shard_map/reshape | solution.py:347
  13.5 0.0 copy-done.2
  13.5 0.0 copy-done.3
  13.6 0.0 copy-done.4
  13.6 29.7 %sparse_conv.1 = (bf16[512,128]{1,0:T(8,128)(2,1)}, bf16[4608,128]{1,0:T(8,128)(2,1)S(1)}, f32[16,128,128]{2,1,0:T(8,128)S(1)}, bf16[4,256,128]{2,1,0:T(8,128)(2,1)S(1)}) custom-call(s32[27,16]{1,0:T(8,128)S(1)} %fusion.1.src, bf16[24,128,128]{2,1,0:T(8,128)(2,1)S(1)} %halo.1.table, bf16[128,3456]{1,0:T(8,128)(2,1)S(1)} %copy.12.wflat, ...), custom_call_target="tpu_custom_call" | custom-call | tf_op jit(solution)/shard_map/sparse_conv/pallas_call | solution.py:350
  43.3 26.8 %reduce.1 = (bf16[4608,128]{1,0:T(8,128)(2,1)S(1)}, f32[16,128,128]{2,1,0:T(8,128)S(1)}) custom-call(bf16[4608,128]{1,0:T(8,128)(2,1)S(1)} %get-tuple-element.11.part, bf16[4,256,128]{2,1,0:T(8,128)(2,1)S(1)} %get-tuple-element.12.halo, f32[16,128,128]{2,1,0:T(8,128)S(1)} %get-tuple-element.13.base, s32[1,1024]{1,0:T(1,128)S(1)} %bitcast.18), custom_call_target="tpu_custom_call" | custom-call | tf_op jit(solution)/shard_map/reduce/pallas_call | solution.py:383
  70.1 0.8 %slice.9 = f32[1024,128]{1,0:T(8,128)} slice(bf16[4608,128]{1,0:T(8,128)(2,1)S(1)} %get-tuple-element.15), slice={[3456:4480], [0:128]} | slice | bytes 1048576 | tf_op jit(solution)/shard_map/slice | solution.py:406
  71.0 1.3 %slice.8 = f32[3456,128]{1,0:T(8,128)} slice(bf16[4608,128]{1,0:T(8,128)(2,1)S(1)} %get-tuple-element.15), slice={[0:3456], [0:128]} | slice | bytes 3538944 | tf_op jit(solution)/shard_map/slice | solution.py:405
  72.3 1.0 %copy.16 = f32[2048,128]{1,0:T(8,128)} copy(f32[2048,128]{1,0:T(8,128)S(1)} %bitcast.15) | data formatting | bytes 2097152
  (1 shorter events, 0.0 us)
Async XLA Ops:
  0.6 11.8 %copy-start = (bf16[27,128,128]{2,1,0:T(8,128)(2,1)S(1)}, bf16[27,128,128]{2,1,0:T(8,128)(2,1)}, u32[]{:S(2)}) copy-start(bf16[27,128,128]{2,1,0:T(8,128)(2,1)} %weight.1) | copy-start | bytes 2654212
  3.0 1.0 %copy-start.1 = (bf16[2048,128]{1,0:T(8,128)(2,1)S(1)}, bf16[2048,128]{1,0:T(8,128)(2,1)}, u32[]{:S(2)}) copy-start(bf16[2048,128]{1,0:T(8,128)(2,1)} %param.7) | copy-start | bytes 1572868
  12.5 1.0 %copy-start.2 = (bf16[8,128,128]{2,1,0:T(8,128)(2,1)S(1)}, bf16[8,128,128]{2,1,0:T(8,128)(2,1)}, u32[]{:S(2)}) copy-start(bf16[8,128,128]{2,1,0:T(8,128)(2,1)} %down.1) | copy-start | bytes 786436
  12.5 1.0 %copy-start.3 = (bf16[512,128]{1,0:T(8,128)(2,1)S(1)}, bf16[512,128]{1,0:T(8,128)(2,1)}, u32[]{:S(2)}) copy-start(bf16[512,128]{1,0:T(8,128)(2,1)} %cgrad.1) | copy-start | bytes 393220
  12.5 1.0 %copy-start.4 = (s32[2048]{0:T(1024)S(1)}, s32[2048]{0:T(1024)}, u32[]{:S(2)}) copy-start(s32[2048]{0:T(1024)} %param.13) | copy-start | bytes 24580

commit v5 on v4

--- a/solution.py
+++ b/solution.py
@@ -37,7 +37,7 @@
     coarse, part, local_grad, halo_grad,
     ext_grad, gathered, pre_grad, sums, spread, children,
 ):
-    kernels, blocks = book.shape[0], book.shape[1]
+    kernels, blocks = src.shape
     childs, _, quarter, chans = spread.shape
     pairs = blocks // 2
     group = sums.shape[0]
@@ -48,7 +48,7 @@
         spread[s] = one.astype(BF16).reshape(blocks, quarter, chans)
 
     def pick(k, b):
-        return hot(BLOCK, book[k, pl.ds(b, 1), :] - src[k, b] * BLOCK)
+        return hot(BLOCK, book[b, pl.ds(k, 1), :] - src[k, b] * BLOCK)
 
     def pair_of(k, p):
         return jnp.concatenate([table[src[k, 2 * p]], table[src[k, 2 * p + 1]]], axis=1)
@@ -176,7 +176,7 @@
             make(d, sign, src.at[d], dst.at[d]).wait_recv()
 
 
-def halo_kernel(slab, tile, features, lists, table, outgoing, arrived, send, recv):
+def halo_kernel(slab, tile, features, lists, weight, book, table, wflat, source, split, outgoing, arrived, send, recv):
     blocks = features.shape[0]
     per_list = outgoing.shape[1]
     arrived[...] = jnp.zeros_like(arrived)
@@ -193,6 +193,17 @@
             outgoing[d, j] = picked[:, j * BLOCK : (j + 1) * BLOCK]
     pl.semaphore_wait(barrier, neighbour_count(slab, tile))
     send_all(slab, tile, (send, recv), 1, outgoing, arrived)
+    kernels = weight.shape[0]
+    for k in range(kernels):
+        wflat[:, k * BLOCK : (k + 1) * BLOCK] = weight[k].astype(F32).T.astype(BF16)
+    columns = lax.broadcasted_iota(jnp.int32, source.shape, 1)
+    lowest = jnp.zeros(source.shape, F32)
+    for n in range(blocks):
+        own = book[:, n * BLOCK : (n + 1) * BLOCK]
+        split[n] = own
+        one = own.astype(F32)
+        lowest = jnp.where(columns == n, jnp.min(one, axis=1, keepdims=True), lowest)
+    source[...] = jnp.minimum(lowest.astype(jnp.int32) >> 7, table.shape[0] - 1)
     wait_all(slab, tile, (send, recv), 1, outgoing, arrived)
     for d in range(4):
         for j in range(per_list):
@@ -328,11 +339,16 @@
     vmem = pl.BlockSpec(memory_space=pltpu.VMEM)
     lists = boundary_rows.reshape(1, 4 * list_len)
 
-    table = pl.pallas_call(
+    table, wflat, src, book = pl.pallas_call(
         functools.partial(halo_kernel, slab, tile),
-        out_shape=jax.ShapeDtypeStruct((total_blocks, chans, BLOCK), BF16),
-        in_specs=[vmem] * 2,
-        out_specs=vmem,
+        out_shape=(
+            jax.ShapeDtypeStruct((total_blocks, chans, BLOCK), BF16),
+            jax.ShapeDtypeStruct((out_chans, kernels * chans), BF16),
+            jax.ShapeDtypeStruct((kernels, blocks), jnp.int32),
+            jax.ShapeDtypeStruct((blocks, kernels, BLOCK), jnp.int32),
+        ),
+        in_specs=[vmem] * 4,
+        out_specs=(vmem,) * 4,
         scratch_shapes=[
             pltpu.VMEM((4, per_list, chans, BLOCK), BF16),
             pltpu.VMEM((4, per_list, chans, BLOCK), BF16),
@@ -343,10 +359,7 @@
             collective_id=0, has_side_effects=True, vmem_limit_bytes=32 * 2**20
         ),
         name="halo",
-    )(features.reshape(blocks, BLOCK, chans), lists)
-    wflat = conv_weight.transpose(2, 0, 1).reshape(out_chans, kernels * chans)
-    book = rulebook.reshape(kernels, blocks, BLOCK)
-    src = jnp.minimum(jnp.min(book, axis=2) // BLOCK, total_blocks - 1)
+    )(features.reshape(blocks, BLOCK, chans), lists, conv_weight, rulebook)
     coarse, part, local_grad, halo_grad = pl.pallas_call(
         main_kernel,
         out_shape=(

time: 73.5 us -> 73 us (level)
    unnamed x13 -> x16, local copies, waits for them, and re-layouts: 3.8 us -> 4.84 us
    reshape x1 -> x0, local copies, waits for them, and re-layouts: 1 us -> none  [body(): wflat = conv_weight.transpose(2, 0, 1).reshape(out_chans, kernels * chans)]
where the time goes in v5:
time: 73 us; the launch traced here: 72.7 us
  Pallas kernels  65 us (89%)
  local copies, waits for them, and re-layouts  6.99 us (10%)
    pallas_call x1, Pallas kernels, body(): pl.pallas_call(main_kernel, out_shape=(jax.ShapeDtypeStruct((coarse_rows,...  29.8 us
    pallas_call x1, Pallas kernels, body(): pl.pallas_call(functools.partial(reduce_kernel, slab, tile, pieces), out_...  26.8 us
    pallas_call x1, Pallas kernels, body(): pl.pallas_call(functools.partial(halo_kernel, slab, tile), out_shape=(jax...  8.44 us
    unnamed x16, local copies, waits for them, and re-layouts  4.84 us

profile of v5, /device:TPU:0, one launch (start us, length us, event | category | flops | bytes accessed | tf_op | source)
XLA Modules:
  0.0 72.7 jit_solution(1428854771551187280)
XLA Ops:
  0.6 0.0 copy-start.6
  0.6 0.7 copy.11
  1.3 0.0 copy-start
  1.3 1.2 %copy-done = bf16[27,128,128]{2,1,0:T(8,128)(2,1)S(1)} copy-done((bf16[27,128,128]{2,1,0:T(8,128)(2,1)S(1)}, bf16[27,128,128]{2,1,0:T(8,128)(2,1)}, u32[]{:S(2)}) %copy-start) | copy-done | bytes 884760
  2.5 0.0 copy-start.2
  2.5 1.0 %copy-done.2 = bf16[2048,128]{1,0:T(8,128)(2,1)S(1)} copy-done((bf16[2048,128]{1,0:T(8,128)(2,1)S(1)}, bf16[2048,128]{1,0:T(8,128)(2,1)}, u32[]{:S(2)}) %copy-start.2) | copy-done | bytes 524312
  3.5 0.0 copy-start.3
  3.6 0.9 %copy-done.3 = s32[27,2048]{1,0:T(8,128)S(1)} copy-done((s32[27,2048]{1,0:T(8,128)S(1)}, s32[27,2048]{1,0:T(8,128)}, u32[]{:S(2)}) %copy-start.3) | copy-done | bytes 221208
  4.5 0.0 copy-start.1
  4.5 0.0 copy-start.4
  4.5 0.0 copy-start.5
  4.5 8.4 %halo.1 = (bf16[24,128,128]{2,1,0:T(8,128)(2,1)S(1)}, bf16[128,3456]{1,0:T(8,128)(2,1)S(1)}, s32[27,16]{1,0:T(8,128)S(1)}, s32[16,27,128]{2,1,0:T(8,128)S(1)}) custom-call(bf16[16,128,128]{2,1,0:T(8,128)(2,1)S(1)} %bitcast.9, s32[1,1024]{1,0:T(1,128)S(1)} %bitcast.10, bf16[27,128,128]{2,1,0:T(8,128)(2,1)S(1)} %copy-done, s32[27,2048]{1,0:T(8,128)S(1)} %copy-done.3), custom_call_target="tpu_custom_call" | custom-call | tf_op jit(solution)/shard_map/halo/pallas_call | solution.py:342
  13.0 0.0 copy-done.6
  13.0 0.0 copy-done.1
  13.0 0.0 copy-done.4
  13.0 0.0 copy-done.5
  13.0 29.8 %sparse_conv.1 = (bf16[512,128]{1,0:T(8,128)(2,1)}, bf16[4608,128]{1,0:T(8,128)(2,1)S(1)}, f32[16,128,128]{2,1,0:T(8,128)S(1)}, bf16[4,256,128]{2,1,0:T(8,128)(2,1)S(1)}) custom-call(s32[27,16]{1,0:T(8,128)S(1)} %get-tuple-element.14.src, bf16[24,128,128]{2,1,0:T(8,128)(2,1)S(1)} %get-tuple-element.15.table, bf16[128,3456]{1,0:T(8,128)(2,1)S(1)} %get-tuple-element.16.wflat, ...), custom_call_target="tpu_custom_call" | custom-call | tf_op jit(solution)/shard_map/sparse_conv/pallas_call | solution.py:363
  42.8 26.8 %reduce.1 = (bf16[4608,128]{1,0:T(8,128)(2,1)S(1)}, f32[16,128,128]{2,1,0:T(8,128)S(1)}) custom-call(bf16[4608,128]{1,0:T(8,128)(2,1)S(1)} %get-tuple-element.19.part, bf16[4,256,128]{2,1,0:T(8,128)(2,1)S(1)} %get-tuple-element.20.halo, f32[16,128,128]{2,1,0:T(8,128)S(1)} %get-tuple-element.21.base, s32[1,1024]{1,0:T(1,128)S(1)} %bitcast.11), custom_call_target="tpu_custom_call" | custom-call | tf_op jit(solution)/shard_map/reduce/pallas_call | solution.py:396
  69.6 0.8 %slice.9 = f32[1024,128]{1,0:T(8,128)} slice(bf16[4608,128]{1,0:T(8,128)(2,1)S(1)} %get-tuple-element.23), slice={[3456:4480], [0:128]} | slice | bytes 1048576 | tf_op jit(solution)/shard_map/slice | solution.py:419
  70.4 1.3 %slice.8 = f32[3456,128]{1,0:T(8,128)} slice(bf16[4608,128]{1,0:T(8,128)(2,1)S(1)} %get-tuple-element.23), slice={[0:3456], [0:128]} | slice | bytes 3538944 | tf_op jit(solution)/shard_map/slice | solution.py:418
  71.7 1.0 %copy.13 = f32[2048,128]{1,0:T(8,128)} copy(f32[2048,128]{1,0:T(8,128)S(1)} %bitcast.8) | data formatting | bytes 2097152
Async XLA Ops:
  0.6 12.3 %copy-start.6 = (s32[2048]{0:T(1024)S(1)}, s32[2048]{0:T(1024)}, u32[]{:S(2)}) copy-start(s32[2048]{0:T(1024)} %param.13) | copy-start | bytes 24580
  1.3 1.2 %copy-start = (bf16[27,128,128]{2,1,0:T(8,128)(2,1)S(1)}, bf16[27,128,128]{2,1,0:T(8,128)(2,1)}, u32[]{:S(2)}) copy-start(bf16[27,128,128]{2,1,0:T(8,128)(2,1)} %weight.3) | copy-start | bytes 2654212
  2.5 1.0 %copy-start.2 = (bf16[2048,128]{1,0:T(8,128)(2,1)S(1)}, bf16[2048,128]{1,0:T(8,128)(2,1)}, u32[]{:S(2)}) copy-start(bf16[2048,128]{1,0:T(8,128)(2,1)} %param.7) | copy-start | bytes 1572868
  3.5 0.9 %copy-start.3 = (s32[27,2048]{1,0:T(8,128)S(1)}, s32[27,2048]{1,0:T(8,128)}, u32[]{:S(2)}) copy-start(s32[27,2048]{1,0:T(8,128)} %book.1) | copy-start | bytes 663556
  4.5 8.5 %copy-start.1 = (bf16[27,128,128]{2,1,0:T(8,128)(2,1)S(1)}, bf16[27,128,128]{2,1,0:T(8,128)(2,1)}, u32[]{:S(2)}) copy-start(bf16[27,128,128]{2,1,0:T(8,128)(2,1)} %weight.3) | copy-start | bytes 2654212
  4.5 8.5 %copy-start.4 = (bf16[8,128,128]{2,1,0:T(8,128)(2,1)S(1)}, bf16[8,128,128]{2,1,0:T(8,128)(2,1)}, u32[]{:S(2)}) copy-start(bf16[8,128,128]{2,1,0:T(8,128)(2,1)} %down.1) | copy-start | bytes 786436
  4.5 8.5 %copy-start.5 = (bf16[512,128]{1,0:T(8,128)(2,1)S(1)}, bf16[512,128]{1,0:T(8,128)(2,1)}, u32[]{:S(2)}) copy-start(bf16[512,128]{1,0:T(8,128)(2,1)} %cgrad.1) | copy-start | bytes 393220
